TPU v7x, 256 devices: a whole 4x4x8 slice. The times are simulated.
256 devices in a mesh: shot: 64 (over x, z, core), inline: 4 (over y).
Axes of the slice: x: 4, y: 4, z: 8, core: 2. Of those that a mesh axis runs over, the one named last changes fastest.
Arguments:
- traces: bfloat16 [262144, 2, 1536], P(('shot', 'inline')), may hold values from -6 to 6
- fold_bins: int32 [262144, 1], P(('shot', 'inline')), may hold values from 0 to 1023, as said below
- radii: int32 [12], replicated, may hold values from 1 to 8
Outputs:
- similarity: float32 [8, 512, 41, 1536], P('inline', 'shot')
Inputs may be any that keep to these rules, and one draw needn't show every extreme that they name: `fold_bins`: in each device's 1024 traces no bin appears more than 3 times, and some bin appears exactly 3 times.
All inputs are finite; a program needn't handle non-finite values.
Results may differ from a plain program's by a relative error of at most 0.0003.
Values may be sent and summed in bfloat16 or wider, within the bound.
A program may use at most 192 MiB of HBM per device.

v0:
```python
import jax
import jax.numpy as jnp
from jax import lax
from jax.sharding import PartitionSpec as P

NT = 1536
LAGR = 20
TBLK = 128
RT_MAX = 8
RS = 2
IL_DEV = 2
XL_DEV = 8


EPS = 1e-06


def with_halo(cells, sides, width):
    for axis, dim in sides:
        count = lax.axis_size(axis)
        ends = count - 1
        head = lax.slice_in_dim(cells, 0, width, axis=dim)
        tail = lax.slice_in_dim(cells, cells.shape[dim] - width, cells.shape[dim], axis=dim)
        cells = jnp.concatenate(
            [
                lax.ppermute(tail, axis, [(i, (i + 1) % count) for i in range(ends)]),
                cells,
                lax.ppermute(head, axis, [((i + 1) % count, i) for i in range(ends)]),
            ],
            axis=dim,
        )
    return cells


def time_weights(radii):
    radius_t = jnp.repeat(radii, TBLK).astype(jnp.float32)
    offsets = jnp.abs(jnp.arange(-RT_MAX, RT_MAX + 1)).astype(jnp.float32)
    return (
        jnp.maximum(radius_t[None, :] + 1.0 - offsets[:, None], 0.0)
        / ((radius_t + 1.0) ** 2)[None, :]
    )


def temporal_smoother(values, weights):
    padded = jnp.pad(values, [(0, 0)] * (values.ndim - 1) + [(RT_MAX, RT_MAX)])
    summed = weights[0] * padded[..., 0:NT]
    for offset in range(1, 2 * RT_MAX + 1):
        summed = summed + weights[offset] * padded[..., offset : offset + NT]
    return summed


def space_smooth(values, along):
    span_len = values.shape[along] - 2 * RS
    summed = None
    for offset in range(2 * RS + 1):
        weight = (RS + 1 - abs(offset - RS)) / float((RS + 1) ** 2)
        piece = weight * lax.slice_in_dim(values, offset, offset + span_len, axis=along)
        summed = piece if summed is None else summed + piece
    return summed


def lag_products(stack_grid, first_lag, last_lag):
    baseline = stack_grid[:, :, 0]
    monitor = stack_grid[:, :, 1]
    monitor_padded_volume = jnp.pad(monitor, ((0, 0), (0, 0), (LAGR, LAGR)))
    lagged = jnp.stack(
        [
            monitor_padded_volume[..., LAGR + shift_by : LAGR + shift_by + NT]
            for shift_by in range(first_lag, last_lag)
        ],
        axis=2,
    )
    return (baseline[:, :, None] * lagged, lagged * lagged)


def shards(traces, fold_bins, radii):
    n_shot = lax.axis_size("shot")
    bins_dev = IL_DEV * XL_DEV
    bins_tile = bins_dev * n_shot
    trace_count = traces.shape[0]
    trace_rows = traces.reshape(trace_count, 2 * NT)
    bin_ids = fold_bins[:, 0]
    onehot = (bin_ids[:, None] == jnp.arange(bins_tile, dtype=jnp.int32)[None, :]).astype(jnp.int32)
    counts_local = jnp.sum(onehot, axis=0)
    partial_sums = jnp.dot(
        onehot.T.astype(jnp.bfloat16), trace_rows, preferred_element_type=jnp.float32
    )
    stacked_sums, fold_count = (
        lax.psum_scatter(partial_sums, "shot", scatter_dimension=0, tiled=True),
        lax.psum_scatter(counts_local.astype(jnp.float32), "shot", scatter_dimension=0, tiled=True),
    )
    stacks = stacked_sums / jnp.maximum(fold_count, 1.0)[:, None]
    stack_grid = jnp.transpose(stacks.reshape(XL_DEV, IL_DEV, 2, NT), (1, 0, 2, 3))
    weights = time_weights(radii)
    nlag = 2 * LAGR + 1
    cross_term, menergy = lag_products(stack_grid, -LAGR, LAGR + 1)
    baseline = stack_grid[:, :, 0]
    volumes = jnp.concatenate([cross_term, menergy, (baseline * baseline)[:, :, None]], axis=2)
    volumes = temporal_smoother(volumes, weights)
    extended = with_halo(volumes, (("inline", 0),), RS)
    volumes = space_smooth(extended, 0)
    extended = with_halo(volumes, (("shot", 1),), RS)
    volumes = space_smooth(extended, 1)
    benergy = volumes[:, :, 2 * nlag : 2 * nlag + 1]
    return volumes[:, :, 0:nlag] / jnp.sqrt(
        (benergy + EPS) * (volumes[:, :, nlag : 2 * nlag] + EPS)
    )


def solution(mesh):
    placed = (P(("shot", "inline"), None, None), P(("shot", "inline"), None), P())
    return jax.shard_map(
        shards,
        mesh=mesh,
        in_specs=placed,
        out_specs=P("inline", "shot", None, None),
        check_vma=False,
    )
```

profile of v0, /device:TPU:1, one launch (start us, length us, event | category | flops | bytes accessed | tf_op | source)
XLA Modules:
  0.0 535.4 jit_solution(14522750702973569363)
XLA Ops:
  6.5 4.4 copy.97
  11.0 9.0 %fusion.32 = f32[1024,3072]{1,0:T(8,128)} fusion(bf16[1024,3072]{1,0:T(8,128)(2,1)S(1)} %bitcast.100, s32[1024]{0:T(1024)S(1)} %bitcast.103), kind=kOutput, calls=%fused_computation.54 | convolution fusion | flops 6445596672 | bytes 18878464 | tf_op jit(solution)/shard_map/dot_general | solution.py:85
  21.9 129.0 %all-reduce.2 = f32[1024]{0:T(1024)S(1)} all-reduce(f32[1024]{0:T(1024)S(1)} %convert_element_type.40), channel_id=3, replica_groups=mesh['shot'=64,'inline'=4] {'shot'}, use_global_device_ids=true, to_apply=%region_2.0.clone | all-reduce | flops 1024 | bytes 8192
  151.5 29.3 %reduce-scatter.2.cloned.1.call-done = f32[16,3072]{1,0:T(8,128)} async-done(((f32[1024,3072]{1,0:T(8,128)}), f32[16,3072]{1,0:T(8,128)}) %reduce-scatter.2.cloned.1.call-update) | async-done | bytes 196624 | tf_op jit(solution)/shard_map/reduce_scatter | solution.py:89
  180.8 1.0 broadcast_divide_fusion
  185.9 1.2 broadcast_multiply_fusion
  187.1 3.5 pad_maximum_fusion.4
  190.6 85.8 %multiply_add_fusion = f32[2,8,83,1536]{3,1,0,2:T(8,128)} fusion(f32[2,8,83,1536]{3,1,0,2:T(8,128)} %pad_maximum_fusion.4, f32[1536]{0:T(1024)S(1)} %get-tuple-element.6, f32[1536]{0:T(1024)S(1)} %get-tuple-element.7, f32[1536]{0:T(1024)S(1)} %get-tuple-element.8, f32[1536]{0:T(1024)S(1)} %get-tuple-element.9, f32[1536]{0:T(1024)S(1)} %get-tuple-element.10, ...), kind=kLoop, calls=%fused_computation.25 | loop fusion | flops 67313664 | bytes 16422912 | tf_op jit(solution)/shard_map/add | solution.py:48
  276.5 1.3 collective-permute-start.1
  277.8 7.2 %collective-permute-start = (f32[2,8,83,1536]{3,1,0,2:T(8,128)}, f32[2,8,83,1536]{3,1,0,2:T(8,128)}, u32[]{:S(2)}, u32[]{:S(2)}) collective-permute-start(f32[2,8,83,1536]{3,1,0,2:T(8,128)} %multiply_add_fusion), channel_id=1, source_target_pairs={{0,1},{1,2},{2,3},{4,5},{5,6},{6,7},{8,9},{9,10},{10,11},{12,13},{... | collective-permute-start | bytes 24477704 | tf_op jit(solution)/shard_map/ppermute | solution.py:26
  285.0 166.5 %collective-permute-done.1 = f32[2,8,83,1536]{3,1,0,2:T(8,128)} collective-permute-done((f32[2,8,83,1536]{3,1,0,2:T(8,128)}, f32[2,8,83,1536]{3,1,0,2:T(8,128)}, u32[]{:S(2)}, u32[]{:S(2)}) %collective-permute-start.1) | collective-permute-done | bytes 8159264 | tf_op jit(solution)/shard_map/ppermute | solution.py:28
  451.5 0.9 collective-permute-done
  452.4 18.5 %fusion.12 = f32[2,8,83,1536]{3,1,0,2:T(8,128)} fusion(f32[2,8,83,1536]{3,1,0,2:T(8,128)} %collective-permute-done.1, f32[2,8,83,1536]{3,1,0,2:T(8,128)} %multiply_add_fusion, f32[2,8,83,1536]{3,1,0,2:T(8,128)} %collective-permute-done), kind=kLoop, calls=%fused_computation.19 | loop fusion | flops 22437888 | bytes 32636928 | tf_op jit(solution)/shard_map/add | solution.py:58
  470.9 7.9 %fusion.35 = (f32[2,2,83,1536]{3,1,0,2:T(2,128)S(1)}, f32[2,2,83,1536]{3,1,0,2:T(2,128)S(1)}) fusion(f32[2,8,83,1536]{3,1,0,2:T(8,128)} %fusion.12), kind=kLoop, calls=%fused_computation.128 | loop fusion | bytes 8159232 | tf_op jit(solution)/shard_map/slice | solution.py:23
  478.7 0.7 copy.94
  479.4 7.5 %collective-permute-start.3 = (f32[2,2,83,1536]{3,2,1,0:T(8,128)S(1)}, f32[2,2,83,1536]{3,2,1,0:T(8,128)S(1)}, u32[]{:S(2)}, u32[]{:S(2)}) collective-permute-start(f32[2,2,83,1536]{3,2,1,0:T(8,128)S(1)} %copy.94), channel_id=1, source_target_pairs={{4,0},{8,4},{12,8},{16,12},{20,16},{24,20},{28,24},{32,28},{36,32}... | collective-permute-start | bytes 6119432 | tf_op jit(solution)/shard_map/ppermute | solution.py:28
  487.6 2.3 collective-permute-start.2
  489.9 21.0 %collective-permute-done.3 = f32[2,2,83,1536]{3,2,1,0:T(8,128)S(1)} collective-permute-done((f32[2,2,83,1536]{3,2,1,0:T(8,128)S(1)}, f32[2,2,83,1536]{3,2,1,0:T(8,128)S(1)}, u32[]{:S(2)}, u32[]{:S(2)}) %collective-permute-start.3) | collective-permute-done | bytes 2039840 | tf_op jit(solution)/shard_map/ppermute | solution.py:28
  510.9 1.6 copy.95
  512.5 0.8 collective-permute-done.2
  513.3 2.9 copy.93
  516.2 9.2 %fusion.3 = f32[2,8,83,1536]{3,1,0,2:T(8,128)S(1)} fusion(f32[2,8,83,1536]{3,1,0,2:T(8,128)S(1)} %bitcast.98, f32[2,2,83,1536]{3,1,0,2:T(2,128)S(1)} %copy.95, f32[2,2,83,1536]{3,1,0,2:T(2,128)} %copy.93), kind=kLoop, calls=%fused_computation.7 | loop fusion | flops 26517504 | bytes 20398080 | tf_op jit(solution)/shard_map/add | solution.py:58
  525.4 0.9 fusion.31
  526.3 2.2 copy.96
  (69 shorter events, 6.3 us)
Async XLA Ops:
  6.5 174.3 %reduce-scatter.2.cloned.1.call-start = ((), (), s32[]{:S(2)}) async-start(), calls=%async_computation.1 | async-start | bytes 12779520 | tf_op jit(solution)/shard_map/reduce_scatter | solution.py:89
  6.5 4.4 copy-start
  20.0 0.7 copy-start.2
  20.0 131.0 %copy-start.1 = (s32[12]{0:T(128)S(1)}, s32[12]{0:T(128)}, u32[]{:S(2)}) copy-start(s32[12]{0:T(128)} %param.5) | copy-start | bytes 148
  276.5 175.0 %collective-permute-start.1 = (f32[2,8,83,1536]{3,1,0,2:T(8,128)}, f32[2,8,83,1536]{3,1,0,2:T(8,128)}, u32[]{:S(2)}, u32[]{:S(2)}) collective-permute-start(f32[2,8,83,1536]{3,1,0,2:T(8,128)} %multiply_add_fusion), channel_id=1, source_target_pairs={{1,0},{2,1},{3,2},{5,4},{6,5},{7,6},{9,8},{10,9},{11,10},{13,12},{... | collective-permute-start | bytes 24477704 | tf_op jit(solution)/shard_map/ppermute | solution.py:28
  277.8 174.6 %collective-permute-start = (f32[2,8,83,1536]{3,1,0,2:T(8,128)}, f32[2,8,83,1536]{3,1,0,2:T(8,128)}, u32[]{:S(2)}, u32[]{:S(2)}) collective-permute-start(f32[2,8,83,1536]{3,1,0,2:T(8,128)} %multiply_add_fusion), channel_id=1, source_target_pairs={{0,1},{1,2},{2,3},{4,5},{5,6},{6,7},{8,9},{9,10},{10,11},{12,13},{... | collective-permute-start | bytes 24477704 | tf_op jit(solution)/shard_map/ppermute | solution.py:26
  478.7 37.5 %slice-start = ((s8[8159232]{0:T(1024)(128)(4,1)}), s8[4194304]{0:T(1024)(128)(4,1)S(1)}, s32[]{:S(2)}) async-start(s8[8159232]{0:T(1024)(128)(4,1)} %bitcast.97), calls=%async_computation.2 | async-start | bytes 8388608
  479.4 31.5 %collective-permute-start.3 = (f32[2,2,83,1536]{3,2,1,0:T(8,128)S(1)}, f32[2,2,83,1536]{3,2,1,0:T(8,128)S(1)}, u32[]{:S(2)}, u32[]{:S(2)}) collective-permute-start(f32[2,2,83,1536]{3,2,1,0:T(8,128)S(1)} %copy.94), channel_id=1, source_target_pairs={{4,0},{8,4},{12,8},{16,12},{20,16},{24,20},{28,24},{32,28},{36,32}... | collective-permute-start | bytes 6119432 | tf_op jit(solution)/shard_map/ppermute | solution.py:28
  486.9 29.3 %slice-start.1 = ((s8[8159232]{0:T(1024)(128)(4,1)}), s8[3964928]{0:T(1024)(128)(4,1)S(1)}, s32[]{:S(2)}) async-start(s8[8159232]{0:T(1024)(128)(4,1)} %bitcast.97), calls=%async_computation.3 | async-start | bytes 7929856
  487.6 25.7 %collective-permute-start.2 = (f32[2,2,83,1536]{3,2,1,0:T(8,128)S(1)}, f32[2,2,83,1536]{3,2,1,0:T(8,128)S(1)}, u32[]{:S(2)}, u32[]{:S(2)}) collective-permute-start(f32[2,2,83,1536]{3,2,1,0:T(8,128)S(1)} %copy.92), channel_id=1, source_target_pairs={{0,4},{4,8},{8,12},{12,16},{16,20},{20,24},{24,28},{28,32},{32,36}... | collective-permute-start | bytes 6119432 | tf_op jit(solution)/shard_map/ppermute | solution.py:26
Sparse Core Ops, SparseCore 0:
  20.1 160.6 reduce-scatter.1
where the time goes:
time: 542 us; the launch traced here: 535 us
  waiting for transfers between devices  219 us (40%)
  blocking collectives  129 us (24%)
  other arithmetic  121 us (22%)
  local copies, waits for them, and re-layouts  25.1 us (5%)
  starting transfers between devices  18.3 us (3%)
  between operations  14.6 us (3%)
  matrix products  9 us (2%)
    ppermute x2, waiting for transfers between devices, with_halo(): lax.ppermute(head, axis, [((i + 1) % count, i) for i in range(ends)])  187 us
    unnamed x1, blocking collectives  129 us
    add x1, other arithmetic, temporal_smoother(): summed = summed + weights[offset] * padded[..., offset:offset + NT]  85.8 us
    reduce_scatter x1, waiting for transfers between devices, shards(): lax.psum_scatter(partial_sums, 'shot', scatter_dimension=0, tiled=True)  29.3 us
    add x2, other arithmetic, space_smooth(): summed = piece if summed is None else summed + piece  27.7 us
  transfers between devices with their start and end apart: 5, of which 5 were waited for; matrix products, arithmetic and copies ran while one was open for 1% of the time, Pallas kernels for 0%

commit v1 on v0

v1 whole, which is shorter than its diff:
```python
import jax
import jax.numpy as jnp
from jax import lax
from jax.experimental import pallas as pl
from jax.experimental.pallas import tpu as pltpu
from jax.sharding import PartitionSpec as P

NT = 1536
LAGR = 20
NLAG = 2 * LAGR + 1
TBLK = 128
NBLK = NT // TBLK
RT_MAX = 8
RS = 2
IL_DEV = 2
XL_DEV = 8
EPS = 1e-06

IL_H = IL_DEV + 2 * RS
XL_H = XL_DEV + 2 * RS
BINS = IL_DEV * XL_DEV
BINS_H = IL_H * XL_H
OCT = 6
LANES = 128
EDGE = LANES + LANES // 2
WIDE = NT + 2 * EDGE
BAND = 288


def band_matrices(radii):
    row = jnp.arange(2)[:, None] * 8 + jnp.arange(BAND)[None, :] - 84
    offset = jnp.abs(row[None, :, :, None] - jnp.arange(TBLK)[None, None, None, :])
    weight = jnp.maximum(radii[:, None, None, None] + 1 - offset, 0)
    sample = jnp.arange(NBLK)[:, None, None] * TBLK + row[None]
    inside = (sample >= 0) & (sample < NT)
    return jnp.where(inside[..., None], weight, 0).astype(jnp.bfloat16)


def triangle(cells):
    count = len(cells)
    pair = [cells[i] + cells[i + 1] for i in range(count - 1)]
    box = [pair[i] + cells[i + 2] for i in range(count - 2)]
    pair = [box[i] + box[i + 1] for i in range(count - 3)]
    return [pair[i] + box[i + 2] for i in range(count - 4)]


def space_smooth(cell):
    columns = [triangle([cell(il, xl) for il in range(IL_H)]) for xl in range(XL_H)]
    return [triangle([columns[xl][il] for xl in range(XL_H)]) for il in range(IL_DEV)]


def split_store(ref, rows, value):
    high = value.astype(jnp.bfloat16)
    ref[0, rows, LANES:] = high
    ref[1, rows, LANES:] = (value - high.astype(jnp.float32)).astype(jnp.bfloat16)


def similarity_kernel(eps_ref, bm_ref, band_ref, out_ref, base, turned, lagged, smooth, bsmooth, bline, bscale):
    step = pl.program_id(0)

    def tile(which, index):
        return bm_ref[which, :, pl.ds(pl.multiple_of((step + index) * LANES, LANES), LANES)]

    lane = lax.broadcasted_iota(jnp.int32, (8, LANES), 1)
    sub = lax.broadcasted_iota(jnp.int32, (8, LANES), 0)
    source = (lane + sub) % LANES
    stays = lane + sub < LANES

    def turn(row):
        return jnp.take_along_axis(jnp.broadcast_to(row, (8, LANES)), source, axis=1)

    @pl.when(step == 0)
    def _():
        for row in range(BINS_H):
            turned[row] = turn(bm_ref[1, row:row + 1, LANES:2 * LANES])

    later = tile(1, 2)
    for row in range(BINS_H):
        fresh = turn(later[row:row + 1, :])
        lagged[row] = jnp.where(stays, turned[row], fresh)
        turned[row] = fresh

    lanes = lax.broadcasted_iota(jnp.int32, (BINS_H, LANES), 1)
    for octet in range(OCT):
        shift = 8 * octet - LAGR
        if shift > 0:
            mixed = jnp.where(lanes < LANES - shift, tile(0, 1), tile(0, 0))
        else:
            mixed = jnp.where(lanes >= -shift, tile(0, 1), tile(0, 2))
        base[octet] = pltpu.roll(mixed, shift % LANES, axis=1)

    smooth[:, :, :LANES] = smooth[:, :, LANES:]
    bsmooth[:, :, :LANES] = bsmooth[:, :, LANES:]
    for octet in range(OCT + 1):
        def cell(il, xl):
            row = il * XL_H + xl
            moved = lagged[row]
            if octet == OCT:
                return moved * moved
            return base[octet, row:row + 1, :] * moved
        for il, cells in enumerate(space_smooth(cell)):
            for xl in range(0, XL_DEV, 2):
                first = octet * 8 * BINS + (il * XL_DEV + xl) * 8
                split_store(smooth, slice(first, first + 16), jnp.concatenate([cells[xl], cells[xl + 1]], axis=0))

    energy = [base[3, il * XL_H:(il + 1) * XL_H, :] for il in range(IL_H)]
    energy = triangle([value * value for value in energy])
    for il in range(IL_DEV):
        bline[il, :XL_H, :] = energy[il]
    parts = [triangle([bline[il, k:k + XL_DEV, :] for k in range(2 * RS + 1)])[0] for il in range(IL_DEV)]
    split_store(bsmooth, slice(0, BINS), jnp.concatenate(parts, axis=0))

    @pl.when(step > 0)
    def _():
        eps = eps_ref[jnp.maximum(step - 1, 0)]

        def smoothed(ref, rows, band):
            return jnp.dot(ref[0, rows, :], band, preferred_element_type=jnp.float32) + jnp.dot(
                ref[1, rows, :], band, preferred_element_type=jnp.float32
            )

        def band_of(octet):
            start = 40 - 8 * octet
            return band_ref[0, (start // 8) % 2, start // 16 * 16:start // 16 * 16 + 2 * LANES, :]

        bscale[...] = lax.rsqrt(smoothed(bsmooth, slice(0, BINS), band_of(3)) + eps)
        for octet in range(OCT):
            band = band_of(octet)
            cross = smoothed(smooth, slice(octet * 8 * BINS, (octet + 1) * 8 * BINS), band)
            menergy = smoothed(smooth, slice(OCT * 8 * BINS, (OCT + 1) * 8 * BINS), band)
            value = cross * lax.rsqrt(menergy + eps)
            value = value.reshape(IL_DEV, XL_DEV, 8, LANES)
            value = value * bscale[...].reshape(IL_DEV, XL_DEV, 1, LANES)
            count = min(8, NLAG - 8 * octet)
            out_ref[:, :, 8 * octet:8 * octet + count, :] = value[:, :, :count, :]


def similarity(bm, radii):
    eps = EPS * 81.0 * (radii.astype(jnp.float32) + 1.0) ** 2
    return pl.pallas_call(
        similarity_kernel,
        grid=(NBLK + 1,),
        out_shape=jax.ShapeDtypeStruct((IL_DEV, XL_DEV, NLAG, NT), jnp.float32),
        in_specs=[
            pl.BlockSpec(memory_space=pltpu.SMEM),
            pl.BlockSpec((2, BINS_H, WIDE), lambda j: (0, 0, 0)),
            pl.BlockSpec((1, 2, BAND, TBLK), lambda j: (jnp.maximum(j - 1, 0), 0, 0, 0)),
        ],
        out_specs=pl.BlockSpec((IL_DEV, XL_DEV, NLAG, TBLK), lambda j: (0, 0, 0, jnp.maximum(j - 1, 0))),
        scratch_shapes=[
            pltpu.VMEM((OCT, BINS_H, LANES), jnp.float32),
            pltpu.VMEM((BINS_H, 8, LANES), jnp.float32),
            pltpu.VMEM((BINS_H, 8, LANES), jnp.float32),
            pltpu.VMEM((2, (OCT + 1) * 8 * BINS, 2 * LANES), jnp.bfloat16),
            pltpu.VMEM((2, BINS, 2 * LANES), jnp.bfloat16),
            pltpu.VMEM((IL_DEV, 16, LANES), jnp.float32),
            pltpu.VMEM((BINS, LANES), jnp.float32),
        ],
        compiler_params=pltpu.CompilerParams(vmem_limit_bytes=48 << 20),
        name="similarity",
    )(eps, bm, band_matrices(radii))


def with_halo(cells, sides, width):
    for axis, dim in sides:
        count = lax.axis_size(axis)
        ends = count - 1
        head = lax.slice_in_dim(cells, 0, width, axis=dim)
        tail = lax.slice_in_dim(cells, cells.shape[dim] - width, cells.shape[dim], axis=dim)
        cells = jnp.concatenate(
            [
                lax.ppermute(tail, axis, [(i, (i + 1) % count) for i in range(ends)]),
                cells,
                lax.ppermute(head, axis, [((i + 1) % count, i) for i in range(ends)]),
            ],
            axis=dim,
        )
    return cells


def shards(traces, fold_bins, radii):
    n_shot = lax.axis_size("shot")
    bins_dev = IL_DEV * XL_DEV
    bins_tile = bins_dev * n_shot
    trace_count = traces.shape[0]
    trace_rows = traces.reshape(trace_count, 2 * NT)
    bin_ids = fold_bins[:, 0]
    onehot = (bin_ids[:, None] == jnp.arange(bins_tile, dtype=jnp.int32)[None, :]).astype(jnp.int32)
    counts_local = jnp.sum(onehot, axis=0)
    partial_sums = jnp.dot(
        onehot.T.astype(jnp.bfloat16), trace_rows, preferred_element_type=jnp.float32
    )
    stacked_sums, fold_count = (
        lax.psum_scatter(partial_sums, "shot", scatter_dimension=0, tiled=True),
        lax.psum_scatter(counts_local.astype(jnp.float32), "shot", scatter_dimension=0, tiled=True),
    )
    stacks = stacked_sums / jnp.maximum(fold_count, 1.0)[:, None]
    stack_grid = jnp.transpose(stacks.reshape(XL_DEV, IL_DEV, 2, NT), (1, 0, 2, 3))
    haloed = with_halo(stack_grid, (("inline", 0), ("shot", 1)), RS)
    bm = jnp.transpose(haloed.reshape(BINS_H, 2, NT), (1, 0, 2))
    bm = jnp.pad(bm, ((0, 0), (0, 0), (EDGE, EDGE)))
    return similarity(bm, radii)


def solution(mesh):
    placed = (P(("shot", "inline"), None, None), P(("shot", "inline"), None), P())
    return jax.shard_map(
        shards,
        mesh=mesh,
        in_specs=placed,
        out_specs=P("inline", "shot", None, None),
        check_vma=False,
    )
```

time: 542 us -> 237 us (0.44); the launches traced: 535 us -> 236 us
  waiting for transfers between devices: 219 us -> 37.3 us
  other arithmetic: 121 us -> 3.93 us
  Pallas kernels: 0 us -> 15.7 us
  local copies, waits for them, and re-layouts: 25.1 us -> 12.4 us
    ppermute x2, waiting for transfers between devices: 187 us -> 8.01 us  [with_halo(): lax.ppermute(head, axis, [((i + 1) % count, i) for i in range(ends)])]
    add x4 -> x1, other arithmetic: 114 us -> 0.01 us  [band_matrices(): weight = jnp.maximum(radii[:, None, None, None] + 1 - offset, 0)]
    pallas_call x0 -> x1, Pallas kernels: none -> 15.7 us  [similarity(): pl.pallas_call(similarity_kernel, grid=(NBLK + 1,), out_shape=jax.ShapeDt...]
    slice x4 -> x0, local copies, waits for them, and re-layouts: 9.47 us -> none  [the longest x2 8.53 us: with_halo(): lax.slice_in_dim(cells, cells.shape[dim] - width, cells.shape[dim], axis=...]
    pallas_call x0 -> x1, local copies, waits for them, and re-layouts: none -> 6.63 us  [similarity(): pl.pallas_call(similarity_kernel, grid=(NBLK + 1,), out_shape=jax.ShapeDt...]
    ppermute x2, starting transfers between devices: 8.78 us -> 3.21 us  [with_halo(): lax.ppermute(head, axis, [((i + 1) % count, i) for i in range(ends)])]
  transfers between devices with their start and end apart: 5 -> 5, of which waited for: 5 -> 4; matrix products, arithmetic and copies ran while one was open for 1% -> 1% of each run, Pallas kernels for 0% -> 0%
where the time goes in v1:
time: 237 us; the launch traced here: 236 us
  blocking collectives  129 us (54%)
  waiting for transfers between devices  37.3 us (16%)
  Pallas kernels  15.7 us (7%)
  starting transfers between devices  14.5 us (6%)
  between operations  14.2 us (6%)
  local copies, waits for them, and re-layouts  12.4 us (5%)
  matrix products  9.2 us (4%)
  other arithmetic  3.93 us (2%)
    unnamed x1, blocking collectives  129 us
    reduce_scatter x1, waiting for transfers between devices, shards(): lax.psum_scatter(partial_sums, 'shot', scatter_dimension=0, tiled=True)  29.1 us
    pallas_call x1, Pallas kernels, similarity(): pl.pallas_call(similarity_kernel, grid=(NBLK + 1,), out_shape=jax.ShapeDt...  15.7 us
    ppermute x2, starting transfers between devices, with_halo(): lax.ppermute(tail, axis, [(i, (i + 1) % count) for i in range(ends)])  11.3 us
    dot_general x1, matrix products, shards(): jnp.dot(onehot.T.astype(jnp.bfloat16), trace_rows, preferred_element_type...  9.2 us
    ppermute x2, waiting for transfers between devices, with_halo(): lax.ppermute(head, axis, [((i + 1) % count, i) for i in range(ends)])  8.01 us
    pallas_call x1, local copies, waits for them, and re-layouts, similarity(): pl.pallas_call(similarity_kernel, grid=(NBLK + 1,), out_shape=jax.ShapeDt...  6.63 us
    unnamed x8, local copies, waits for them, and re-layouts  5.15 us
  transfers between devices with their start and end apart: 5, of which 4 were waited for; matrix products, arithmetic and copies ran while one was open for 1% of the time, Pallas kernels for 0%

profile of v1, /device:TPU:1, one launch (start us, length us, event | category | flops | bytes accessed | tf_op | source)
XLA Modules:
  0.0 236.3 jit_solution(2166785198554132685)
XLA Ops:
  6.5 4.4 %copy.15 = bf16[128,8,2,1536]{3,1,2,0:T(8,128)(2,1)S(1)} copy(bf16[128,8,2,1536]{3,2,1,0:T(2,128)(2,1)} %bitcast.12) | data formatting | bytes 12582912
  11.0 9.2 %fusion = f32[1024,3072]{1,0:T(8,128)} fusion(bf16[1024,3072]{1,0:T(8,128)(2,1)S(1)} %bitcast.13, s32[1024]{0:T(1024)S(1)} %bitcast.20), kind=kOutput, calls=%fused_computation.5 | convolution fusion | flops 6445596672 | bytes 18878464 | tf_op jit(solution)/shard_map/dot_general | solution.py:190
  20.2 0.5 convert_reduce_fusion
  20.7 0.1 copy-done.2
  20.9 0.6 dynamic-slice
  22.1 128.9 %all-reduce.1 = f32[1024]{0:T(1024)S(1)} all-reduce(f32[1024]{0:T(1024)S(1)} %convert_element_type.24), channel_id=3, replica_groups=mesh['shot'=64,'inline'=4] {'shot'}, use_global_device_ids=true, to_apply=%region_2.0.clone | all-reduce | flops 1024 | bytes 8192
  151.3 0.1 subtract_abs_fusion
  151.5 29.1 %reduce-scatter.2.cloned.1.call-done = f32[16,3072]{1,0:T(8,128)} async-done(((f32[1024,3072]{1,0:T(8,128)}), f32[16,3072]{1,0:T(8,128)}) %reduce-scatter.2.cloned.1.call-update) | async-done | bytes 196624 | tf_op jit(solution)/shard_map/reduce_scatter | solution.py:194
  180.6 1.0 broadcast_divide_fusion
  181.6 0.2 reshape.79
  181.8 3.1 %collective-permute-start = (f32[2,8,2,1536]{3,2,1,0:T(2,128)S(1)}, f32[2,8,2,1536]{3,2,1,0:T(2,128)S(1)}, u32[]{:S(2)}, u32[]{:S(2)}) collective-permute-start(f32[2,8,2,1536]{3,2,1,0:T(2,128)S(1)} %bitcast.16), channel_id=1, source_target_pairs={{0,1},{1,2},{2,3},{4,5},{5,6},{6,7},{8,9},{9,10},{10,11},{12,13},{... | collective-permute-start | bytes 589832 | tf_op jit(solution)/shard_map/ppermute | solution.py:172
  184.9 1.3 collective-permute-start.1
  186.2 1.5 select_convert_fusion.band_ref
  187.7 3.6 %collective-permute-done.1 = f32[2,8,2,1536]{3,2,1,0:T(2,128)S(1)} collective-permute-done((f32[2,8,2,1536]{3,2,1,0:T(2,128)S(1)}, f32[2,8,2,1536]{3,2,1,0:T(2,128)S(1)}, u32[]{:S(2)}, u32[]{:S(2)}) %collective-permute-start.1) | collective-permute-done | bytes 196640 | tf_op jit(solution)/shard_map/ppermute | solution.py:174
  191.3 0.2 pad_maximum_fusion.3
  191.5 8.2 %collective-permute-start.2 = (f32[6,2,2,1536]{3,2,1,0:T(2,128)S(1)}, f32[6,2,2,1536]{3,2,1,0:T(2,128)S(1)}, u32[]{:S(2)}, u32[]{:S(2)}) collective-permute-start(f32[6,2,2,1536]{3,2,1,0:T(2,128)S(1)} %get-tuple-element.5), channel_id=1, source_target_pairs={{0,4},{4,8},{8,12},{12,16},{16,20},{20,24},{24,28},{28,32},{32,36}... | collective-permute-start | bytes 442376 | tf_op jit(solution)/shard_map/ppermute | solution.py:172
  199.7 1.9 collective-permute-start.3
  201.6 0.1 collective-permute-done.2
  201.8 4.4 %collective-permute-done.3 = f32[6,2,2,1536]{3,2,1,0:T(2,128)S(1)} collective-permute-done((f32[6,2,2,1536]{3,2,1,0:T(2,128)S(1)}, f32[6,2,2,1536]{3,2,1,0:T(2,128)S(1)}, u32[]{:S(2)}, u32[]{:S(2)}) %collective-permute-start.3) | collective-permute-done | bytes 147488 | tf_op jit(solution)/shard_map/ppermute | solution.py:174
  206.1 0.4 pad_maximum_fusion
  206.5 0.2 copy.18
  206.7 0.3 pad.4.bm_ref
  207.0 15.7 %similarity.1 = f32[2,8,41,1536]{3,2,1,0:T(8,128)} custom-call(f32[12]{0:T(128)S(1)} %multiply_multiply_fusion.eps_ref, f32[2,72,1920]{2,1,0:T(8,128)S(1)} %pad.4.bm_ref, bf16[12,2,288,128]{3,2,1,0:T(8,128)(2,1)S(1)} %select_convert_fusion.band_ref), custom_call_target="tpu_custom_call" | custom-call | tf_op jit(solution)/shard_map/similarity/pallas_call | solution.py:140
  222.8 6.6 %copy.14 = f32[2,8,41,1536]{3,1,2,0:T(8,128)} copy(f32[2,8,41,1536]{3,2,1,0:T(8,128)} %similarity.1) | data formatting | bytes 8060928 | tf_op jit(solution)/shard_map/similarity/pallas_call | solution.py:140
  (17 shorter events, 0.3 us)
Async XLA Ops:
  6.5 174.1 %reduce-scatter.2.cloned.1.call-start = ((), (), s32[]{:S(2)}) async-start(), calls=%async_computation.1 | async-start | bytes 12779520 | tf_op jit(solution)/shard_map/reduce_scatter | solution.py:194
  6.5 4.4 %copy-start = (s32[1024,1]{0,1:T(1,128)S(1)}, s32[1024,1]{0,1:T(1,128)}, u32[]{:S(2)}) copy-start(s32[1024,1]{0,1:T(1,128)} %param.4) | copy-start | bytes 12292
  20.2 0.7 copy-start.2
  20.2 130.9 %copy-start.1 = (s32[12]{0:T(128)S(1)}, s32[12]{0:T(128)}, u32[]{:S(2)}) copy-start(s32[12]{0:T(128)} %param.5) | copy-start | bytes 148
  181.8 5.9 %collective-permute-start = (f32[2,8,2,1536]{3,2,1,0:T(2,128)S(1)}, f32[2,8,2,1536]{3,2,1,0:T(2,128)S(1)}, u32[]{:S(2)}, u32[]{:S(2)}) collective-permute-start(f32[2,8,2,1536]{3,2,1,0:T(2,128)S(1)} %bitcast.16), channel_id=1, source_target_pairs={{0,1},{1,2},{2,3},{4,5},{5,6},{6,7},{8,9},{9,10},{10,11},{12,13},{... | collective-permute-start | bytes 589832 | tf_op jit(solution)/shard_map/ppermute | solution.py:172
  184.9 6.4 %collective-permute-start.1 = (f32[2,8,2,1536]{3,2,1,0:T(2,128)S(1)}, f32[2,8,2,1536]{3,2,1,0:T(2,128)S(1)}, u32[]{:S(2)}, u32[]{:S(2)}) collective-permute-start(f32[2,8,2,1536]{3,2,1,0:T(2,128)S(1)} %bitcast.17), channel_id=1, source_target_pairs={{1,0},{2,1},{3,2},{5,4},{6,5},{7,6},{9,8},{10,9},{11,10},{13,12},{... | collective-permute-start | bytes 589832 | tf_op jit(solution)/shard_map/ppermute | solution.py:174
  191.5 10.3 %collective-permute-start.2 = (f32[6,2,2,1536]{3,2,1,0:T(2,128)S(1)}, f32[6,2,2,1536]{3,2,1,0:T(2,128)S(1)}, u32[]{:S(2)}, u32[]{:S(2)}) collective-permute-start(f32[6,2,2,1536]{3,2,1,0:T(2,128)S(1)} %get-tuple-element.5), channel_id=1, source_target_pairs={{0,4},{4,8},{8,12},{12,16},{16,20},{20,24},{24,28},{28,32},{32,36}... | collective-permute-start | bytes 442376 | tf_op jit(solution)/shard_map/ppermute | solution.py:172
  199.7 6.5 %collective-permute-start.3 = (f32[6,2,2,1536]{3,2,1,0:T(2,128)S(1)}, f32[6,2,2,1536]{3,2,1,0:T(2,128)S(1)}, u32[]{:S(2)}, u32[]{:S(2)}) collective-permute-start(f32[6,2,2,1536]{3,2,1,0:T(2,128)S(1)} %get-tuple-element.6), channel_id=1, source_target_pairs={{4,0},{8,4},{12,8},{16,12},{20,16},{24,20},{28,24},{32,28},{36,32}... | collective-permute-start | bytes 442376 | tf_op jit(solution)/shard_map/ppermute | solution.py:174
Sparse Core Ops, SparseCore 0:
  20.3 160.2 reduce-scatter.1

commit v2 on v1

--- a/solution.py
+++ b/solution.py
@@ -1,3 +1,5 @@
+import functools
+
 import jax
 import jax.numpy as jnp
 from jax import lax
@@ -161,44 +163,276 @@
     )(eps, bm, band_matrices(radii))
 
 
-def with_halo(cells, sides, width):
-    for axis, dim in sides:
-        count = lax.axis_size(axis)
-        ends = count - 1
-        head = lax.slice_in_dim(cells, 0, width, axis=dim)
-        tail = lax.slice_in_dim(cells, cells.shape[dim] - width, cells.shape[dim], axis=dim)
-        cells = jnp.concatenate(
-            [
-                lax.ppermute(tail, axis, [(i, (i + 1) % count) for i in range(ends)]),
-                cells,
-                lax.ppermute(head, axis, [((i + 1) % count, i) for i in range(ends)]),
-            ],
-            axis=dim,
+MESH = pl.DeviceIdType.MESH
+RING_X = 4
+CHUNK = 2 * LANES
+X_FIRST = (0, 1, 3, 5, 6, 8, 10)
+PACE = 2
+
+
+def chunk_order(chunks, last):
+    pairs = [(chunk + PACE * op, op, chunk) for chunk in range(chunks) for op in range(last + 1)]
+    return [(chunk, op) for _, op, chunk in sorted(pairs)]
+
+
+def stack_kernel(sizes, ids_ref, rows_ref, out_ref, peer_ids, peer, hot, hot_peer, part, count, count_in, x_big, z_big,
+                 x_small, z_small, y_in, s_in, s_out, own, fold, pair_sem, ring_sem, count_sem, y_sem, s_sem):
+    chunks, nx, nz, ny = sizes
+    shot = lax.axis_index("shot")
+    line = lax.axis_index("inline")
+    n_shot = 2 * nx * nz
+    core = shot % 2
+    mx = shot // (2 * nz)
+    mz = (shot // 2) % nz
+    extent = {"x": nx, "z": nz}
+    place = {"x": mx, "z": mz}
+
+    def along(axis, by):
+        if axis == "x":
+            return ((mx + by + nx) % nx) * (2 * nz) + mz * 2 + core
+        return mx * (2 * nz) + ((mz + by + nz) % nz) * 2 + core
+
+    pair = shot + 1 - 2 * core
+    partners = [(pair, line)]
+    partners += [(along(axis, by), line) for axis in "xz" for by in (1, -1)]
+    partners += [(shot, (line + 1) % ny), (shot, (line + ny - 1) % ny)]
+    partners += [((shot + 1) % n_shot, line), ((shot + n_shot - 1) % n_shot, line)]
+    barrier = pltpu.get_barrier_semaphore()
+    for partner in partners:
+        pl.semaphore_signal(barrier, inc=1, device_id=partner, device_id_type=MESH)
+    pl.semaphore_wait(barrier, len(partners))
+
+    sent = []
+
+    def send(source, target, sems, index, device, when=None):
+        copy = pltpu.make_async_remote_copy(
+            src_ref=source, dst_ref=target, send_sem=sems.at[(0, *index)], recv_sem=sems.at[(1, *index)],
+            device_id=device, device_id_type=MESH,
         )
-    return cells
+        if when is None:
+            copy.start()
+        else:
+            pl.when(when)(copy.start)
+        sent.append((copy, when))
+        return copy
+
+    def arrive(buffer, sems, index, when=None):
+        copy = pltpu.make_async_remote_copy(
+            src_ref=buffer, dst_ref=buffer, send_sem=sems.at[(0, *index)], recv_sem=sems.at[(1, *index)],
+            device_id=(pair, line), device_id_type=MESH,
+        )
+        if when is None:
+            copy.wait_recv()
+        else:
+            pl.when(when)(copy.wait_recv)
+
+    send(ids_ref, peer_ids, pair_sem, (chunks,), (pair, line))
+    for chunk in range(chunks):
+        send(rows_ref.at[chunk], peer.at[chunk], pair_sem, (chunk,), (pair, line))
+
+    @pl.when(line == 0)
+    def _():
+        y_in[0] = jnp.zeros_like(y_in[0])
+
+    @pl.when(line == ny - 1)
+    def _():
+        y_in[1] = jnp.zeros_like(y_in[1])
+
+    @pl.when(shot == 0)
+    def _():
+        s_in[0] = jnp.zeros_like(s_in[0])
+
+    @pl.when(shot == n_shot - 1)
+    def _():
+        s_in[1] = jnp.zeros_like(s_in[1])
+
+    out_ref[...] = jnp.zeros_like(out_ref)
+
+    bins = nx * nz * BINS
+
+    def one_hot(ids, target):
+        def block(i, carry):
+            row = lax.broadcasted_iota(jnp.int32, (32, 1), 0) + i * 32
+            cell = row % BINS
+            name = (row // BINS) * (2 * BINS) + core * BINS + (cell % XL_DEV) * IL_DEV + cell // XL_DEV
+            target[pl.ds(pl.multiple_of(i * 32, 32), 32), :] = jnp.where(ids == name, 1.0, 0.0).astype(jnp.bfloat16)
+            return carry
+        lax.fori_loop(0, bins // 32, block, 0)
+
+    one_hot(ids_ref[...], hot)
+    arrive(peer_ids, pair_sem, (chunks,))
+    one_hot(peer_ids[...], hot_peer)
+
+    contract = (((1,), (1,)), ((), ()))
+    ones = jnp.ones((8, hot.shape[1]), jnp.bfloat16)
+    wide = nz * BINS
+    sub = lax.broadcasted_iota(jnp.int32, (8, wide), 0)
+    tile = jnp.zeros((8, wide), jnp.float32)
+    for x in range(nx):
+        counted = sum(
+            lax.dot_general(ones, ref[x * wide:(x + 1) * wide, :], contract, preferred_element_type=jnp.float32)
+            for ref in (hot, hot_peer)
+        )
+        tile = jnp.where(sub == x, counted, tile)
+    count[0] = tile
+
+    def ring(axis, sems, index, local, inbox, step, turn):
+        n = extent[axis]
+        hops = (n // 2, n - 1 - n // 2)
+        for way in range(2):
+            if step > 0 and step <= hops[way]:
+                arrive(inbox(way, step - 1), sems, (*index, way, step - 1))
+            if step < hops[way]:
+                toward = turn if way == 0 else -turn
+                dest = (place[axis] + toward * (hops[way] - step) + n) % n
+                source = local(dest)
+                if step > 0:
+                    held = inbox(way, step - 1)
+                    held[...] = held[...] + source[...]
+                    source = held
+                send(source, inbox(way, step), sems, (*index, way, step), (along(axis, toward), line))
+
+    def settled(axis, inbox):
+        n = extent[axis]
+        return sum(inbox(way, hop - 1)[...] for way, hop in enumerate((n // 2, n - 1 - n // 2)) if hop > 0)
+
+    first_x = [chunk for chunk in range(chunks) if chunk in X_FIRST]
+    first_z = [chunk for chunk in range(chunks) if chunk not in X_FIRST]
+    steps_x, steps_z = nx // 2, nz // 2
+
+    def count_op(op):
+        if op <= steps_z:
+            inbox = lambda way, step: count_in.at[0, way, step]
+            ring("z", count_sem, (0,), lambda dest: count.at[0], inbox, op, 1)
+            if op == steps_z:
+                count[1] = count[0] + settled("z", inbox)
+        if op >= steps_z:
+            inbox = lambda way, step: count_in.at[1, way, step]
+            ring("x", count_sem, (1,), lambda dest: count.at[1], inbox, op - steps_z, 1)
+            if op == steps_z + steps_x:
+                total = count[1] + settled("x", inbox)
+                mine = jnp.sum(jnp.where(sub == mx, total, 0.0), axis=0, keepdims=True)
+                lane = lax.broadcasted_iota(jnp.int32, (BINS, wide), 1)
+                cell = lax.broadcasted_iota(jnp.int32, (BINS, wide), 0)
+                mine = jnp.where(lane == mz * BINS + cell, jnp.broadcast_to(mine, (BINS, wide)), 0.0)
+                mine = jnp.sum(mine, axis=1, keepdims=True)
+                fold[...] = jnp.broadcast_to(jnp.maximum(mine, 1.0), fold.shape)
+
+    last = steps_x + steps_z + 2
+
+    def chunk_op(chunk, op):
+        x_leads = chunk in X_FIRST
+        slot = (first_x if x_leads else first_z).index(chunk)
+        turn = 1 if slot % 2 == 0 else -1
+        axes = "xz" if x_leads else "zx"
+        half = steps_x if x_leads else steps_z
+        full = steps_x + steps_z
+        big, small = (x_big, z_small) if x_leads else (z_big, x_small)
+        big_in = lambda way, step: big.at[slot, way, step]
+        small_in = lambda way, step: small.at[slot, way, step]
+        mine = part.at[chunk, mx] if x_leads else part.at[chunk, :, mz]
+        if op == 0:
+            arrive(peer.at[chunk], pair_sem, (chunk,))
+            summed = jnp.dot(hot[...], rows_ref[chunk], preferred_element_type=jnp.float32) + jnp.dot(
+                hot_peer[...], peer[chunk], preferred_element_type=jnp.float32
+            )
+            part[chunk] = summed.reshape(nx, nz, BINS, CHUNK)
+        if op <= half:
+            local = (lambda dest: part.at[chunk, dest]) if x_leads else (lambda dest: part.at[chunk, :, dest])
+            ring(axes[0], ring_sem, (chunk, 0), local, big_in, op, turn)
+            if op == half:
+                mine[...] = mine[...] + settled(axes[0], big_in)
+        if half <= op <= full:
+            local = (lambda dest: part.at[chunk, mx, dest]) if x_leads else (lambda dest: part.at[chunk, dest, mz])
+            ring(axes[1], ring_sem, (chunk, 1), local, small_in, op - half, turn)
+            if op == full:
+                stacks = (part[chunk, mx, mz] + settled(axes[1], small_in)) / fold[:, :1]
+                own[chunk] = stacks
+                send(own.at[chunk], y_in.at[0, chunk], y_sem, (0, chunk), (shot, (line + 1) % ny), line < ny - 1)
+                send(own.at[chunk], y_in.at[1, chunk], y_sem, (1, chunk), (shot, (line + ny - 1) % ny), line > 0)
+        lanes = slice(EDGE + chunk * LANES, EDGE + (chunk + 1) * LANES)
+        if op == full + 1:
+            arrive(y_in.at[0, chunk], y_sem, (0, chunk), line > 0)
+            arrive(y_in.at[1, chunk], y_sem, (1, chunk), line < ny - 1)
+            for group, block in enumerate((y_in[0, chunk], own[chunk], y_in[1, chunk])):
+                for which in range(2):
+                    for il in range(IL_DEV):
+                        cells = block[il * XL_DEV:(il + 1) * XL_DEV, which * LANES:(which + 1) * LANES]
+                        inline = group * IL_DEV + il
+                        out_ref[which, inline * XL_H + RS:inline * XL_H + RS + XL_DEV, lanes] = cells
+                        edge = (which * IL_H + inline) * RS
+                        s_out[0, chunk, edge:edge + RS, :] = cells[XL_DEV - RS:, :]
+                        s_out[1, chunk, edge:edge + RS, :] = cells[:RS, :]
+            send(s_out.at[0, chunk], s_in.at[0, chunk], s_sem, (0, chunk), ((shot + 1) % n_shot, line), shot < n_shot - 1)
+            send(s_out.at[1, chunk], s_in.at[1, chunk], s_sem, (1, chunk), ((shot + n_shot - 1) % n_shot, line), shot > 0)
+        if op == full + 2:
+            arrive(s_in.at[0, chunk], s_sem, (0, chunk), shot > 0)
+            arrive(s_in.at[1, chunk], s_sem, (1, chunk), shot < n_shot - 1)
+            for side in range(2):
+                for which in range(2):
+                    for inline in range(IL_H):
+                        edge = (which * IL_H + inline) * RS
+                        row = inline * XL_H + side * (RS + XL_DEV)
+                        out_ref[which, row:row + RS, lanes] = s_in[side, chunk, edge:edge + RS, :]
+
+    for chunk, op in chunk_order(chunks, last):
+        if chunk == 0 and op <= steps_x + steps_z:
+            count_op(op)
+        chunk_op(chunk, op)
+
+    for copy, when in sent:
+        if when is None:
+            copy.wait_send()
+        else:
+            pl.when(when)(copy.wait_send)
+
+
+def haloed_stacks(rows, ids, n_shot, ny, nx=RING_X):
+    chunks, traces, _ = rows.shape
+    nz = n_shot // (2 * nx)
+    leads = len([chunk for chunk in range(chunks) if chunk in X_FIRST])
+    cells = (BINS, CHUNK)
+    scratch = [
+        pltpu.VMEM((1, traces), jnp.int32),
+        pltpu.VMEM((chunks, traces, CHUNK), jnp.bfloat16),
+        pltpu.VMEM((nx * nz * BINS, traces), jnp.bfloat16),
+        pltpu.VMEM((nx * nz * BINS, traces), jnp.bfloat16),
+        pltpu.VMEM((chunks, nx, nz, *cells), jnp.float32),
+        pltpu.VMEM((2, 8, nz * BINS), jnp.float32),
+        pltpu.VMEM((2, 2, max(nx, nz) // 2, 8, nz * BINS), jnp.float32),
+        pltpu.VMEM((leads, 2, nx // 2, nz, *cells), jnp.float32),
+        pltpu.VMEM((chunks - leads, 2, nz // 2, nx, *cells), jnp.float32),
+        pltpu.VMEM((chunks - leads, 2, nx // 2, *cells), jnp.float32),
+        pltpu.VMEM((leads, 2, nz // 2, *cells), jnp.float32),
+        pltpu.VMEM((2, chunks, *cells), jnp.float32),
+        pltpu.VMEM((2, chunks, 2 * IL_H * RS, LANES), jnp.float32),
+        pltpu.VMEM((2, chunks, 2 * IL_H * RS, LANES), jnp.float32),
+        pltpu.VMEM((chunks, *cells), jnp.float32),
+        pltpu.VMEM((BINS, LANES), jnp.float32),
+        pltpu.SemaphoreType.DMA((2, chunks + 1)),
+        pltpu.SemaphoreType.DMA((2, chunks, 2, 2, max(nx, nz) // 2)),
+        pltpu.SemaphoreType.DMA((2, 2, 2, max(nx, nz) // 2)),
+        pltpu.SemaphoreType.DMA((2, 2, chunks)),
+        pltpu.SemaphoreType.DMA((2, 2, chunks)),
+    ]
+    vmem = pl.BlockSpec(memory_space=pltpu.VMEM)
+    return pl.pallas_call(
+        functools.partial(stack_kernel, (chunks, nx, nz, ny)),
+        out_shape=jax.ShapeDtypeStruct((2, BINS_H, chunks * LANES + 2 * EDGE), jnp.float32),
+        in_specs=[vmem, vmem],
+        out_specs=vmem,
+        scratch_shapes=scratch,
+        compiler_params=pltpu.CompilerParams(
+            collective_id=0, has_side_effects=True, vmem_limit_bytes=56 << 20
+        ),
+        name="stack",
+    )(ids, rows)
 
 
 def shards(traces, fold_bins, radii):
-    n_shot = lax.axis_size("shot")
-    bins_dev = IL_DEV * XL_DEV
-    bins_tile = bins_dev * n_shot
-    trace_count = traces.shape[0]
-    trace_rows = traces.reshape(trace_count, 2 * NT)
-    bin_ids = fold_bins[:, 0]
-    onehot = (bin_ids[:, None] == jnp.arange(bins_tile, dtype=jnp.int32)[None, :]).astype(jnp.int32)
-    counts_local = jnp.sum(onehot, axis=0)
-    partial_sums = jnp.dot(
-        onehot.T.astype(jnp.bfloat16), trace_rows, preferred_element_type=jnp.float32
-    )
-    stacked_sums, fold_count = (
-        lax.psum_scatter(partial_sums, "shot", scatter_dimension=0, tiled=True),
-        lax.psum_scatter(counts_local.astype(jnp.float32), "shot", scatter_dimension=0, tiled=True),
-    )
-    stacks = stacked_sums / jnp.maximum(fold_count, 1.0)[:, None]
-    stack_grid = jnp.transpose(stacks.reshape(XL_DEV, IL_DEV, 2, NT), (1, 0, 2, 3))
-    haloed = with_halo(stack_grid, (("inline", 0), ("shot", 1)), RS)
-    bm = jnp.transpose(haloed.reshape(BINS_H, 2, NT), (1, 0, 2))
-    bm = jnp.pad(bm, ((0, 0), (0, 0), (EDGE, EDGE)))
+    count = traces.shape[0]
+    rows = traces.reshape(count, 2, NBLK, LANES).transpose(2, 0, 1, 3).reshape(NBLK, count, CHUNK)
+    bm = haloed_stacks(rows, fold_bins.reshape(1, count), lax.axis_size("shot"), lax.axis_size("inline"))
     return similarity(bm, radii)
 
 

time: 237 us -> 151 us (0.64)
  blocking collectives: 129 us -> 0 us
  Pallas kernels: 15.7 us -> 96.5 us
  local copies, waits for them, and re-layouts: 12.4 us -> 51 us
  waiting for transfers between devices: 37.3 us -> 0 us
  starting transfers between devices: 14.5 us -> 0 us
  between operations: 14.2 us -> 0.07 us
  matrix products: 9.2 us -> 0 us
    unnamed x1 -> x0, blocking collectives: 129 us -> none
    pallas_call x0 -> x1, Pallas kernels: none -> 80.8 us  [haloed_stacks(): pl.pallas_call(functools.partial(stack_kernel, (chunks, nx, nz, ny)), out...]
    reduce_scatter x1 -> x0, waiting for transfers between devices: 29.1 us -> none  [shards(): lax.psum_scatter(partial_sums, 'shot', scatter_dimension=0, tiled=True)]
    transpose x0 -> x1, local copies, waits for them, and re-layouts: none -> 16.2 us  [shards(): traces.reshape(count, 2, NBLK, LANES).transpose(2, 0, 1, 3)]
    ppermute x4 -> x0, starting transfers between devices: 14.5 us -> none  [the longest x2 11.3 us: with_halo(): lax.ppermute(tail, axis, [(i, (i + 1) % count) for i in range(ends)])]
    unnamed x8 -> x5, local copies, waits for them, and re-layouts: 5.15 us -> 17.4 us
    reshape x3 -> x1, local copies, waits for them, and re-layouts: 0.36 us -> 10.8 us  [shards(): traces.reshape(count, 2, NBLK, LANES).transpose(2, 0, 1, 3)]
    dot_general x1 -> x0, matrix products: 9.2 us -> none  [shards(): jnp.dot(onehot.T.astype(jnp.bfloat16), trace_rows, preferred_element_type...]
  transfers between devices with their start and end apart: 5 -> 0, of which waited for: 4 -> 0; matrix products, arithmetic and copies ran while one was open for 1% -> 0% of each run, Pallas kernels for 0% -> 0%
where the time goes in v2:
time: 151 us; the launch traced here: 150 us
  Pallas kernels  96.5 us (64%)
  local copies, waits for them, and re-layouts  51 us (34%)
  other arithmetic  2.45 us (2%)
    pallas_call x1, Pallas kernels, haloed_stacks(): pl.pallas_call(functools.partial(stack_kernel, (chunks, nx, nz, ny)), out...  80.8 us
    unnamed x5, local copies, waits for them, and re-layouts  17.4 us
    transpose x1, local copies, waits for them, and re-layouts, shards(): traces.reshape(count, 2, NBLK, LANES).transpose(2, 0, 1, 3)  16.2 us
    pallas_call x1, Pallas kernels, similarity(): pl.pallas_call(similarity_kernel, grid=(NBLK + 1,), out_shape=jax.ShapeDt...  15.7 us
    reshape x1, local copies, waits for them, and re-layouts, shards(): traces.reshape(count, 2, NBLK, LANES).transpose(2, 0, 1, 3)  10.8 us
    pallas_call x1, local copies, waits for them, and re-layouts, similarity(): pl.pallas_call(similarity_kernel, grid=(NBLK + 1,), out_shape=jax.ShapeDt...  6.63 us

profile of v2, /device:TPU:1, one launch (start us, length us, event | category | flops | bytes accessed | tf_op | source)
XLA Modules:
  0.0 150.0 jit_solution(7504677228800579461)
XLA Ops:
  0.0 0.7 multiply_multiply_fusion.eps_ref
  0.7 16.1 %copy.6 = bf16[1024,2,1536]{0,2,1:T(8,128)(2,1)} copy(bf16[1024,2,1536]{2,1,0:T(2,128)(2,1)} %param.3) | data formatting | bytes 12582912 | tf_op args[0]
  16.8 16.2 %copy.7 = bf16[12,1024,2,128]{3,2,1,0:T(2,128)(2,1)} copy(bf16[12,1024,2,128]{1,3,0,2:T(8,128)(2,1)} %bitcast.4) | data formatting | bytes 12582912 | tf_op jit(solution)/shard_map/transpose | solution.py:434
  33.0 10.8 %reshape.79.rows_ref = bf16[12,1024,256]{2,1,0:T(8,128)(2,1)} reshape(bf16[12,1024,2,128]{3,2,1,0:T(2,128)(2,1)} %copy.7) | data formatting | bytes 12582912 | tf_op jit(solution)/shard_map/reshape | solution.py:434
  43.8 0.0 copy-start.1
  43.8 80.8 %stack.1.bm_ref = f32[2,72,1920]{2,1,0:T(8,128)} custom-call(s32[1,1024]{1,0:T(1,128)} %bitcast.5, bf16[12,1024,256]{2,1,0:T(8,128)(2,1)} %reshape.79.rows_ref), custom_call_target="tpu_custom_call" | custom-call | tf_op jit(solution)/shard_map/stack/pallas_call | solution.py:419
  124.6 0.1 add_add_fusion
  124.7 0.1 subtract_abs_fusion
  124.8 0.0 copy-done.1
  124.9 0.1 compare_and_fusion
  125.0 1.5 select_convert_fusion.band_ref
  126.4 0.0 copy-start
  126.5 1.2 copy-done
  127.7 15.7 %similarity.1 = f32[2,8,41,1536]{3,2,1,0:T(8,128)} custom-call(f32[12]{0:T(128)S(1)} %multiply_multiply_fusion.eps_ref, f32[2,72,1920]{2,1,0:T(8,128)S(1)} %copy-done, bf16[12,2,288,128]{3,2,1,0:T(8,128)(2,1)S(1)} %select_convert_fusion.band_ref), custom_call_target="tpu_custom_call" | custom-call | tf_op jit(solution)/shard_map/similarity/pallas_call | solution.py:142
  143.4 6.6 %copy.8 = f32[2,8,41,1536]{3,1,2,0:T(8,128)} copy(f32[2,8,41,1536]{3,2,1,0:T(8,128)} %similarity.1) | data formatting | bytes 8060928 | tf_op jit(solution)/shard_map/similarity/pallas_call | solution.py:142
  (3 shorter events, 0.0 us)
Async XLA Ops:
  43.8 81.0 %copy-start.1 = (s32[12]{0:T(128)S(1)}, s32[12]{0:T(128)}, u32[]{:S(2)}) copy-start(s32[12]{0:T(128)} %param.5) | copy-start | bytes 148
  126.4 1.2 copy-start

commit v3 on v2

--- a/solution.py
+++ b/solution.py
@@ -131,24 +131,29 @@
             cross = smoothed(smooth, slice(octet * 8 * BINS, (octet + 1) * 8 * BINS), band)
             menergy = smoothed(smooth, slice(OCT * 8 * BINS, (OCT + 1) * 8 * BINS), band)
             value = cross * lax.rsqrt(menergy + eps)
-            value = value.reshape(IL_DEV, XL_DEV, 8, LANES)
-            value = value * bscale[...].reshape(IL_DEV, XL_DEV, 1, LANES)
+            value = value.reshape(BINS, 8, LANES) * bscale[...].reshape(BINS, 1, LANES)
             count = min(8, NLAG - 8 * octet)
-            out_ref[:, :, 8 * octet:8 * octet + count, :] = value[:, :, :count, :]
+            for cell in range(BINS):
+                il, xl = cell // XL_DEV, cell % XL_DEV
+                if count == 8:
+                    out_ref[il, pl.ds(octet * 8 * XL_DEV + xl, 8, stride=XL_DEV), :] = value[cell]
+                else:
+                    row = octet * 8 * XL_DEV + xl
+                    out_ref[il, row:row + 1, :] = value[cell, :count, :]
 
 
 def similarity(bm, radii):
     eps = EPS * 81.0 * (radii.astype(jnp.float32) + 1.0) ** 2
-    return pl.pallas_call(
+    out = pl.pallas_call(
         similarity_kernel,
         grid=(NBLK + 1,),
-        out_shape=jax.ShapeDtypeStruct((IL_DEV, XL_DEV, NLAG, NT), jnp.float32),
+        out_shape=jax.ShapeDtypeStruct((IL_DEV, NLAG * XL_DEV, NT), jnp.float32),
         in_specs=[
             pl.BlockSpec(memory_space=pltpu.SMEM),
             pl.BlockSpec((2, BINS_H, WIDE), lambda j: (0, 0, 0)),
             pl.BlockSpec((1, 2, BAND, TBLK), lambda j: (jnp.maximum(j - 1, 0), 0, 0, 0)),
         ],
-        out_specs=pl.BlockSpec((IL_DEV, XL_DEV, NLAG, TBLK), lambda j: (0, 0, 0, jnp.maximum(j - 1, 0))),
+        out_specs=pl.BlockSpec((IL_DEV, NLAG * XL_DEV, TBLK), lambda j: (0, 0, jnp.maximum(j - 1, 0))),
         scratch_shapes=[
             pltpu.VMEM((OCT, BINS_H, LANES), jnp.float32),
             pltpu.VMEM((BINS_H, 8, LANES), jnp.float32),
@@ -161,22 +166,23 @@
         compiler_params=pltpu.CompilerParams(vmem_limit_bytes=48 << 20),
         name="similarity",
     )(eps, bm, band_matrices(radii))
+    return jnp.transpose(out.reshape(IL_DEV, NLAG, XL_DEV, NT), (0, 2, 1, 3))
 
 
 MESH = pl.DeviceIdType.MESH
 RING_X = 4
 CHUNK = 2 * LANES
 X_FIRST = (0, 1, 3, 5, 6, 8, 10)
-PACE = 2
-
-
-def chunk_order(chunks, last):
-    pairs = [(chunk + PACE * op, op, chunk) for chunk in range(chunks) for op in range(last + 1)]
-    return [(chunk, op) for _, op, chunk in sorted(pairs)]
+ORDER = (
+    0, 2, 3, 1, 4, 2, 7, 5, 9, 4, 0, 11, 8, 9, 6, 3, 7, 11, 0, 9, 1, 10, 5, 4, 7, 11, 0,
+    6, 2, 4, 7, 8, 1, 3, 11, 2, 10, 4, 9, 7, 3, 5, 6, 0, 1, 8, 2, 11, 9, 3, 10, 6, 4, 1,
+    5, 7, 8, 2, 3, 10, 6, 11, 1, 5, 4, 8, 0, 9, 10, 6, 3, 1, 5, 2, 8, 11, 7, 9, 10, 6, 0,
+    4, 5, 1, 8, 11, 3, 10, 7, 9, 6, 0, 2, 1, 8, 4, 5, 10, 3, 11, 0, 9, 2, 8, 6, 7, 5, 10,
+)
 
 
 def stack_kernel(sizes, ids_ref, rows_ref, out_ref, peer_ids, peer, hot, hot_peer, part, count, count_in, x_big, z_big,
-                 x_small, z_small, y_in, s_in, s_out, own, fold, pair_sem, ring_sem, count_sem, y_sem, s_sem):
+                 x_small, z_small, y_in, s_in, s_out, own, fold, rows, row_sem, pair_sem, ring_sem, count_sem, y_sem, s_sem):
     chunks, nx, nz, ny = sizes
     shot = lax.axis_index("shot")
     line = lax.axis_index("inline")
@@ -200,6 +206,28 @@
     barrier = pltpu.get_barrier_semaphore()
     for partner in partners:
         pl.semaphore_signal(barrier, inc=1, device_id=partner, device_id_type=MESH)
+
+    def block_of(ref, chunk):
+        return ref.at[:, :, chunk * LANES:(chunk + 1) * LANES]
+
+    loads = []
+    for chunk in range(chunks):
+        loads.append(pltpu.make_async_copy(block_of(rows_ref, chunk), block_of(rows, chunk), row_sem.at[chunk]))
+        loads[-1].start()
+
+    bins = nx * nz * BINS
+
+    def one_hot(ids, target):
+        def block(i, carry):
+            row = lax.broadcasted_iota(jnp.int32, (32, 1), 0) + i * 32
+            cell = row % BINS
+            name = (row // BINS) * (2 * BINS) + core * BINS + (cell % XL_DEV) * IL_DEV + cell // XL_DEV
+            target[pl.ds(pl.multiple_of(i * 32, 32), 32), :] = jnp.where(ids == name, 1.0, 0.0).astype(jnp.bfloat16)
+            return carry
+        lax.fori_loop(0, bins // 32, block, 0)
+
+    one_hot(ids_ref[...], hot)
+    out_ref[...] = jnp.zeros_like(out_ref)
     pl.semaphore_wait(barrier, len(partners))
 
     sent = []
@@ -226,9 +254,13 @@
         else:
             pl.when(when)(copy.wait_recv)
 
+    def terms(ref, chunk):
+        block = block_of(ref, chunk)
+        return jnp.concatenate([block[0], block[1]], axis=1)
+
     send(ids_ref, peer_ids, pair_sem, (chunks,), (pair, line))
     for chunk in range(chunks):
-        send(rows_ref.at[chunk], peer.at[chunk], pair_sem, (chunk,), (pair, line))
+        send(block_of(rows_ref, chunk), block_of(peer, chunk), pair_sem, (chunk,), (pair, line))
 
     @pl.when(line == 0)
     def _():
@@ -246,20 +278,6 @@
     def _():
         s_in[1] = jnp.zeros_like(s_in[1])
 
-    out_ref[...] = jnp.zeros_like(out_ref)
-
-    bins = nx * nz * BINS
-
-    def one_hot(ids, target):
-        def block(i, carry):
-            row = lax.broadcasted_iota(jnp.int32, (32, 1), 0) + i * 32
-            cell = row % BINS
-            name = (row // BINS) * (2 * BINS) + core * BINS + (cell % XL_DEV) * IL_DEV + cell // XL_DEV
-            target[pl.ds(pl.multiple_of(i * 32, 32), 32), :] = jnp.where(ids == name, 1.0, 0.0).astype(jnp.bfloat16)
-            return carry
-        lax.fori_loop(0, bins // 32, block, 0)
-
-    one_hot(ids_ref[...], hot)
     arrive(peer_ids, pair_sem, (chunks,))
     one_hot(peer_ids[...], hot_peer)
 
@@ -332,9 +350,10 @@
         small_in = lambda way, step: small.at[slot, way, step]
         mine = part.at[chunk, mx] if x_leads else part.at[chunk, :, mz]
         if op == 0:
-            arrive(peer.at[chunk], pair_sem, (chunk,))
-            summed = jnp.dot(hot[...], rows_ref[chunk], preferred_element_type=jnp.float32) + jnp.dot(
-                hot_peer[...], peer[chunk], preferred_element_type=jnp.float32
+            arrive(block_of(peer, chunk), pair_sem, (chunk,))
+            loads[chunk].wait()
+            summed = jnp.dot(hot[...], terms(rows, chunk), preferred_element_type=jnp.float32) + jnp.dot(
+                hot_peer[...], terms(peer, chunk), preferred_element_type=jnp.float32
             )
             part[chunk] = summed.reshape(nx, nz, BINS, CHUNK)
         if op <= half:
@@ -375,9 +394,16 @@
                         row = inline * XL_H + side * (RS + XL_DEV)
                         out_ref[which, row:row + RS, lanes] = s_in[side, chunk, edge:edge + RS, :]
 
-    for chunk, op in chunk_order(chunks, last):
-        if chunk == 0 and op <= steps_x + steps_z:
+    done = [0] * chunks
+    counted = 0
+    for chunk in [chunk for chunk in ORDER if chunk < chunks]:
+        op = done[chunk]
+        done[chunk] += 1
+        if op > last:
+            continue
+        if op == counted and op <= steps_x + steps_z:
             count_op(op)
+            counted += 1
         chunk_op(chunk, op)
 
     for copy, when in sent:
@@ -388,13 +414,13 @@
 
 
 def haloed_stacks(rows, ids, n_shot, ny, nx=RING_X):
-    chunks, traces, _ = rows.shape
+    traces, chunks = rows.shape[1], rows.shape[2] // LANES
     nz = n_shot // (2 * nx)
     leads = len([chunk for chunk in range(chunks) if chunk in X_FIRST])
     cells = (BINS, CHUNK)
     scratch = [
         pltpu.VMEM((1, traces), jnp.int32),
-        pltpu.VMEM((chunks, traces, CHUNK), jnp.bfloat16),
+        pltpu.VMEM((2, traces, chunks * LANES), jnp.bfloat16),
         pltpu.VMEM((nx * nz * BINS, traces), jnp.bfloat16),
         pltpu.VMEM((nx * nz * BINS, traces), jnp.bfloat16),
         pltpu.VMEM((chunks, nx, nz, *cells), jnp.float32),
@@ -409,6 +435,8 @@
         pltpu.VMEM((2, chunks, 2 * IL_H * RS, LANES), jnp.float32),
         pltpu.VMEM((chunks, *cells), jnp.float32),
         pltpu.VMEM((BINS, LANES), jnp.float32),
+        pltpu.VMEM((2, traces, chunks * LANES), jnp.bfloat16),
+        pltpu.SemaphoreType.DMA((chunks,)),
         pltpu.SemaphoreType.DMA((2, chunks + 1)),
         pltpu.SemaphoreType.DMA((2, chunks, 2, 2, max(nx, nz) // 2)),
         pltpu.SemaphoreType.DMA((2, 2, 2, max(nx, nz) // 2)),
@@ -419,7 +447,7 @@
     return pl.pallas_call(
         functools.partial(stack_kernel, (chunks, nx, nz, ny)),
         out_shape=jax.ShapeDtypeStruct((2, BINS_H, chunks * LANES + 2 * EDGE), jnp.float32),
-        in_specs=[vmem, vmem],
+        in_specs=[vmem, pl.BlockSpec(memory_space=pl.ANY)],
         out_specs=vmem,
         scratch_shapes=scratch,
         compiler_params=pltpu.CompilerParams(
@@ -431,8 +459,7 @@
 
 def shards(traces, fold_bins, radii):
     count = traces.shape[0]
-    rows = traces.reshape(count, 2, NBLK, LANES).transpose(2, 0, 1, 3).reshape(NBLK, count, CHUNK)
-    bm = haloed_stacks(rows, fold_bins.reshape(1, count), lax.axis_size("shot"), lax.axis_size("inline"))
+    bm = haloed_stacks(jnp.transpose(traces, (1, 0, 2)), fold_bins.reshape(1, count), lax.axis_size("shot"), lax.axis_size("inline"))
     return similarity(bm, radii)
 
 

time: 151 us -> 96.1 us (0.64)
  local copies, waits for them, and re-layouts: 51 us -> 7.66 us
  Pallas kernels: 96.5 us -> 85.7 us
    transpose x1 -> x0, local copies, waits for them, and re-layouts: 16.2 us -> none  [shards(): traces.reshape(count, 2, NBLK, LANES).transpose(2, 0, 1, 3)]
    reshape x1 -> x0, local copies, waits for them, and re-layouts: 10.8 us -> none  [shards(): traces.reshape(count, 2, NBLK, LANES).transpose(2, 0, 1, 3)]
    pallas_call x1, Pallas kernels: 80.8 us -> 70.1 us  [haloed_stacks(): pl.pallas_call(functools.partial(stack_kernel, (chunks, nx, nz, ny)), out...]
    unnamed x5, local copies, waits for them, and re-layouts: 17.4 us -> 7.66 us
    pallas_call x1 -> x0, local copies, waits for them, and re-layouts: 6.63 us -> none  [similarity(): pl.pallas_call(similarity_kernel, grid=(NBLK + 1,), out_shape=jax.ShapeDt...]
where the time goes in v3:
time: 96.1 us; the launch traced here: 95.9 us
  Pallas kernels  85.7 us (89%)
  local copies, waits for them, and re-layouts  7.66 us (8%)
  other arithmetic  2.45 us (3%)
    pallas_call x1, Pallas kernels, haloed_stacks(): pl.pallas_call(functools.partial(stack_kernel, (chunks, nx, nz, ny)), out...  70.1 us
    pallas_call x1, Pallas kernels, similarity(): pl.pallas_call(similarity_kernel, grid=(NBLK + 1,), out_shape=jax.ShapeDt...  15.6 us
    unnamed x5, local copies, waits for them, and re-layouts  7.66 us

profile of v3, /device:TPU:1, one launch (start us, length us, event | category | flops | bytes accessed | tf_op | source)
XLA Modules:
  0.0 95.9 jit_solution(18043242870932265006)
XLA Ops:
  0.0 0.7 multiply_multiply_fusion.eps_ref
  0.7 6.4 %copy.6 = bf16[1024,2,1536]{2,0,1:T(8,128)(2,1)} copy(bf16[1024,2,1536]{2,1,0:T(2,128)(2,1)} %param.3) | data formatting | bytes 12582912 | tf_op args[0]
  7.1 0.0 copy-start.1
  7.1 70.1 %stack.1.bm_ref = f32[2,72,1920]{2,1,0:T(8,128)} custom-call(s32[1,1024]{1,0:T(1,128)} %bitcast.8, bf16[2,1024,1536]{2,1,0:T(8,128)(2,1)} %bitcast.7), custom_call_target="tpu_custom_call" | custom-call | tf_op jit(solution)/shard_map/stack/pallas_call | solution.py:447
  77.2 0.1 add_add_fusion
  77.2 0.1 subtract_abs_fusion
  77.4 0.0 copy-done.1
  77.4 0.1 compare_and_fusion
  77.5 1.5 %select_convert_fusion.band_ref = bf16[12,2,288,128]{3,2,1,0:T(8,128)(2,1)S(1)} fusion(s32[2,288,128]{2,1,0:T(8,128)S(1)} %subtract_abs_fusion, s32[12]{0:T(128)S(1)} %broadcast_add_fusion, pred[12,2,288]{2,1,0:T(4,128)(4,1)S(1)} %compare_and_fusion), kind=kLoop, calls=%fused_computation.1 | loop fusion | flops 3538944 | bytes 2071344 | tf_op jit(solution)/shard_map/convert_element_type | solution.py:38
  79.0 0.0 copy-start
  79.0 1.2 %copy-done = f32[2,72,1920]{2,1,0:T(8,128)S(1)} copy-done((f32[2,72,1920]{2,1,0:T(8,128)S(1)}, f32[2,72,1920]{2,1,0:T(8,128)}, u32[]{:S(2)}) %copy-start) | copy-done | bytes 1105944
  80.3 15.6 %similarity.1 = f32[2,328,1536]{2,1,0:T(8,128)} custom-call(f32[12]{0:T(128)S(1)} %multiply_multiply_fusion.eps_ref, f32[2,72,1920]{2,1,0:T(8,128)S(1)} %copy-done, bf16[12,2,288,128]{3,2,1,0:T(8,128)(2,1)S(1)} %select_convert_fusion.band_ref), custom_call_target="tpu_custom_call" | custom-call | tf_op jit(solution)/shard_map/similarity/pallas_call | solution.py:147
  (3 shorter events, 0.0 us)
Async XLA Ops:
  7.1 70.3 %copy-start.1 = (s32[12]{0:T(128)S(1)}, s32[12]{0:T(128)}, u32[]{:S(2)}) copy-start(s32[12]{0:T(128)} %param.5) | copy-start | bytes 148
  79.0 1.2 %copy-start = (f32[2,72,1920]{2,1,0:T(8,128)S(1)}, f32[2,72,1920]{2,1,0:T(8,128)}, u32[]{:S(2)}) copy-start(f32[2,72,1920]{2,1,0:T(8,128)} %stack.1.bm_ref) | copy-start | bytes 3317764

commit v4 on v3

--- a/solution.py
+++ b/solution.py
@@ -57,7 +57,7 @@
     ref[1, rows, LANES:] = (value - high.astype(jnp.float32)).astype(jnp.bfloat16)
 
 
-def similarity_kernel(eps_ref, bm_ref, band_ref, out_ref, base, turned, lagged, smooth, bsmooth, bline, bscale):
+def similarity_kernel(radii_ref, bm_ref, band_ref, out_ref, base, turned, lagged, smooth, bsmooth, bline, bscale):
     step = pl.program_id(0)
 
     def tile(which, index):
@@ -114,7 +114,7 @@
 
     @pl.when(step > 0)
     def _():
-        eps = eps_ref[jnp.maximum(step - 1, 0)]
+        eps = EPS * 81.0 * (radii_ref[jnp.maximum(step - 1, 0)].astype(jnp.float32) + 1.0) ** 2
 
         def smoothed(ref, rows, band):
             return jnp.dot(ref[0, rows, :], band, preferred_element_type=jnp.float32) + jnp.dot(
@@ -142,8 +142,7 @@
                     out_ref[il, row:row + 1, :] = value[cell, :count, :]
 
 
-def similarity(bm, radii):
-    eps = EPS * 81.0 * (radii.astype(jnp.float32) + 1.0) ** 2
+def similarity(bm, bands, radii):
     out = pl.pallas_call(
         similarity_kernel,
         grid=(NBLK + 1,),
@@ -163,9 +162,9 @@
             pltpu.VMEM((IL_DEV, 16, LANES), jnp.float32),
             pltpu.VMEM((BINS, LANES), jnp.float32),
         ],
-        compiler_params=pltpu.CompilerParams(vmem_limit_bytes=48 << 20),
+        compiler_params=pltpu.CompilerParams(vmem_limit_bytes=24 << 20),
         name="similarity",
-    )(eps, bm, band_matrices(radii))
+    )(radii, bm, bands)
     return jnp.transpose(out.reshape(IL_DEV, NLAG, XL_DEV, NT), (0, 2, 1, 3))
 
 
@@ -182,7 +181,7 @@
 
 
 def stack_kernel(sizes, ids_ref, rows_ref, out_ref, peer_ids, peer, hot, hot_peer, part, count, count_in, x_big, z_big,
-                 x_small, z_small, y_in, s_in, s_out, own, fold, rows, row_sem, pair_sem, ring_sem, count_sem, y_sem, s_sem):
+                 x_small, z_small, y_in, s_in, s_out, own, fold, pair_sem, ring_sem, count_sem, y_sem, s_sem):
     chunks, nx, nz, ny = sizes
     shot = lax.axis_index("shot")
     line = lax.axis_index("inline")
@@ -209,11 +208,6 @@
 
     def block_of(ref, chunk):
         return ref.at[:, :, chunk * LANES:(chunk + 1) * LANES]
-
-    loads = []
-    for chunk in range(chunks):
-        loads.append(pltpu.make_async_copy(block_of(rows_ref, chunk), block_of(rows, chunk), row_sem.at[chunk]))
-        loads[-1].start()
 
     bins = nx * nz * BINS
 
@@ -351,8 +345,7 @@
         mine = part.at[chunk, mx] if x_leads else part.at[chunk, :, mz]
         if op == 0:
             arrive(block_of(peer, chunk), pair_sem, (chunk,))
-            loads[chunk].wait()
-            summed = jnp.dot(hot[...], terms(rows, chunk), preferred_element_type=jnp.float32) + jnp.dot(
+            summed = jnp.dot(hot[...], terms(rows_ref, chunk), preferred_element_type=jnp.float32) + jnp.dot(
                 hot_peer[...], terms(peer, chunk), preferred_element_type=jnp.float32
             )
             part[chunk] = summed.reshape(nx, nz, BINS, CHUNK)
@@ -435,8 +428,6 @@
         pltpu.VMEM((2, chunks, 2 * IL_H * RS, LANES), jnp.float32),
         pltpu.VMEM((chunks, *cells), jnp.float32),
         pltpu.VMEM((BINS, LANES), jnp.float32),
-        pltpu.VMEM((2, traces, chunks * LANES), jnp.bfloat16),
-        pltpu.SemaphoreType.DMA((chunks,)),
         pltpu.SemaphoreType.DMA((2, chunks + 1)),
         pltpu.SemaphoreType.DMA((2, chunks, 2, 2, max(nx, nz) // 2)),
         pltpu.SemaphoreType.DMA((2, 2, 2, max(nx, nz) // 2)),
@@ -447,11 +438,11 @@
     return pl.pallas_call(
         functools.partial(stack_kernel, (chunks, nx, nz, ny)),
         out_shape=jax.ShapeDtypeStruct((2, BINS_H, chunks * LANES + 2 * EDGE), jnp.float32),
-        in_specs=[vmem, pl.BlockSpec(memory_space=pl.ANY)],
+        in_specs=[vmem, vmem],
         out_specs=vmem,
         scratch_shapes=scratch,
         compiler_params=pltpu.CompilerParams(
-            collective_id=0, has_side_effects=True, vmem_limit_bytes=56 << 20
+            collective_id=0, has_side_effects=True, vmem_limit_bytes=32 << 20
         ),
         name="stack",
     )(ids, rows)
@@ -459,8 +450,9 @@
 
 def shards(traces, fold_bins, radii):
     count = traces.shape[0]
-    bm = haloed_stacks(jnp.transpose(traces, (1, 0, 2)), fold_bins.reshape(1, count), lax.axis_size("shot"), lax.axis_size("inline"))
-    return similarity(bm, radii)
+    rows, ids = jnp.transpose(traces, (1, 0, 2)), fold_bins.reshape(1, count)
+    bm = haloed_stacks(rows, ids, lax.axis_size("shot"), lax.axis_size("inline"))
+    return similarity(bm, band_matrices(radii), radii)
 
 
 def solution(mesh):

time: 96.1 us -> 90.1 us (0.938)
  local copies, waits for them, and re-layouts: 7.66 us -> 3.79 us
  Pallas kernels: 85.7 us -> 84.4 us
    unnamed x5, local copies, waits for them, and re-layouts: 7.66 us -> 3.79 us
    pallas_call x1, Pallas kernels: 70.1 us -> 68.7 us  [haloed_stacks(): pl.pallas_call(functools.partial(stack_kernel, (chunks, nx, nz, ny)), out...]
where the time goes in v4:
time: 90.1 us; the launch traced here: 90 us
  Pallas kernels  84.4 us (94%)
  local copies, waits for them, and re-layouts  3.79 us (4%)
  other arithmetic  1.79 us (2%)
    pallas_call x1, Pallas kernels, haloed_stacks(): pl.pallas_call(functools.partial(stack_kernel, (chunks, nx, nz, ny)), out...  68.7 us
    pallas_call x1, Pallas kernels, similarity(): pl.pallas_call(similarity_kernel, grid=(NBLK + 1,), out_shape=jax.ShapeDt...  15.6 us
    unnamed x5, local copies, waits for them, and re-layouts  3.79 us

profile of v4, /device:TPU:1, one launch (start us, length us, event | category | flops | bytes accessed | tf_op | source)
XLA Modules:
  0.0 90.0 jit_solution(16560490473233472033)
XLA Ops:
  0.0 0.0 copy-start
  0.0 3.8 %copy.6 = bf16[1024,2,1536]{2,0,1:T(8,128)(2,1)S(1)} copy(bf16[1024,2,1536]{2,1,0:T(2,128)(2,1)} %param.3) | data formatting | bytes 12582912 | tf_op args[0]
  3.8 0.0 copy-done
  3.8 0.0 copy-start.1
  3.8 68.7 %stack.1.bm_ref = f32[2,72,1920]{2,1,0:T(8,128)S(1)} custom-call(s32[1,1024]{1,0:T(1,128)S(1)} %bitcast.8, bf16[2,1024,1536]{2,1,0:T(8,128)(2,1)S(1)} %bitcast.7), custom_call_target="tpu_custom_call" | custom-call | tf_op jit(solution)/shard_map/stack/pallas_call | solution.py:438
  72.5 0.1 add_add_fusion
  72.6 0.1 subtract_abs_fusion
  72.8 0.0 copy-done.1
  72.8 0.1 compare_and_fusion
  72.9 1.5 %select_convert_fusion.band_ref = bf16[12,2,288,128]{3,2,1,0:T(8,128)(2,1)S(1)} fusion(s32[2,288,128]{2,1,0:T(8,128)S(1)} %subtract_abs_fusion, s32[12]{0:T(128)S(1)} %broadcast_add_fusion, pred[12,2,288]{2,1,0:T(4,128)(4,1)S(1)} %compare_and_fusion), kind=kLoop, calls=%fused_computation.1 | loop fusion | flops 3538944 | bytes 2071344 | tf_op jit(solution)/shard_map/convert_element_type | solution.py:38
  74.4 15.6 %similarity.1 = f32[2,328,1536]{2,1,0:T(8,128)} custom-call(s32[12]{0:T(128)S(1)} %copy-done.1, f32[2,72,1920]{2,1,0:T(8,128)S(1)} %stack.1.bm_ref, bf16[12,2,288,128]{3,2,1,0:T(8,128)(2,1)S(1)} %select_convert_fusion.band_ref), custom_call_target="tpu_custom_call" | custom-call | tf_op jit(solution)/shard_map/similarity/pallas_call | solution.py:146
  (3 shorter events, 0.0 us)
Async XLA Ops:
  0.0 3.8 %copy-start = (s32[1024,1]{0,1:T(1,128)S(1)}, s32[1024,1]{0,1:T(1,128)}, u32[]{:S(2)}) copy-start(s32[1024,1]{0,1:T(1,128)} %param.4) | copy-start | bytes 12292
  3.8 69.0 %copy-start.1 = (s32[12]{0:T(128)S(1)}, s32[12]{0:T(128)}, u32[]{:S(2)}) copy-start(s32[12]{0:T(128)} %radii_ref.1) | copy-start | bytes 148

commit v5 on v4

--- a/solution.py
+++ b/solution.py
@@ -53,15 +53,16 @@
 
 def split_store(ref, rows, value):
     high = value.astype(jnp.bfloat16)
-    ref[0, rows, LANES:] = high
-    ref[1, rows, LANES:] = (value - high.astype(jnp.float32)).astype(jnp.bfloat16)
-
-
-def similarity_kernel(radii_ref, bm_ref, band_ref, out_ref, base, turned, lagged, smooth, bsmooth, bline, bscale):
+    ref[0, rows, :] = high
+    ref[1, rows, :] = (value - high.astype(jnp.float32)).astype(jnp.bfloat16)
+
+
+def similarity_kernel(radii_ref, bm_ref, band_ref, out_ref, base, turned, lagged, smooth, bsmooth, newer, bnewer, bline, bscale):
     step = pl.program_id(0)
+    place = jnp.minimum(step, NBLK)
 
     def tile(which, index):
-        return bm_ref[which, :, pl.ds(pl.multiple_of((step + index) * LANES, LANES), LANES)]
+        return bm_ref[which, :, pl.ds(pl.multiple_of((place + index) * LANES, LANES), LANES)]
 
     lane = lax.broadcasted_iota(jnp.int32, (8, LANES), 1)
     sub = lax.broadcasted_iota(jnp.int32, (8, LANES), 0)
@@ -91,9 +92,7 @@
             mixed = jnp.where(lanes >= -shift, tile(0, 1), tile(0, 2))
         base[octet] = pltpu.roll(mixed, shift % LANES, axis=1)
 
-    smooth[:, :, :LANES] = smooth[:, :, LANES:]
-    bsmooth[:, :, :LANES] = bsmooth[:, :, LANES:]
-    for octet in range(OCT + 1):
+    def products(octet):
         def cell(il, xl):
             row = il * XL_H + xl
             moved = lagged[row]
@@ -103,62 +102,72 @@
         for il, cells in enumerate(space_smooth(cell)):
             for xl in range(0, XL_DEV, 2):
                 first = octet * 8 * BINS + (il * XL_DEV + xl) * 8
-                split_store(smooth, slice(first, first + 16), jnp.concatenate([cells[xl], cells[xl + 1]], axis=0))
+                split_store(newer, slice(first, first + 16), jnp.concatenate([cells[xl], cells[xl + 1]], axis=0))
 
     energy = [base[3, il * XL_H:(il + 1) * XL_H, :] for il in range(IL_H)]
     energy = triangle([value * value for value in energy])
     for il in range(IL_DEV):
         bline[il, :XL_H, :] = energy[il]
     parts = [triangle([bline[il, k:k + XL_DEV, :] for k in range(2 * RS + 1)])[0] for il in range(IL_DEV)]
-    split_store(bsmooth, slice(0, BINS), jnp.concatenate(parts, axis=0))
-
-    @pl.when(step > 0)
-    def _():
-        eps = EPS * 81.0 * (radii_ref[jnp.maximum(step - 1, 0)].astype(jnp.float32) + 1.0) ** 2
-
-        def smoothed(ref, rows, band):
-            return jnp.dot(ref[0, rows, :], band, preferred_element_type=jnp.float32) + jnp.dot(
-                ref[1, rows, :], band, preferred_element_type=jnp.float32
-            )
-
-        def band_of(octet):
-            start = 40 - 8 * octet
-            return band_ref[0, (start // 8) % 2, start // 16 * 16:start // 16 * 16 + 2 * LANES, :]
-
-        bscale[...] = lax.rsqrt(smoothed(bsmooth, slice(0, BINS), band_of(3)) + eps)
-        for octet in range(OCT):
-            band = band_of(octet)
-            cross = smoothed(smooth, slice(octet * 8 * BINS, (octet + 1) * 8 * BINS), band)
-            menergy = smoothed(smooth, slice(OCT * 8 * BINS, (OCT + 1) * 8 * BINS), band)
-            value = cross * lax.rsqrt(menergy + eps)
-            value = value.reshape(BINS, 8, LANES) * bscale[...].reshape(BINS, 1, LANES)
-            count = min(8, NLAG - 8 * octet)
-            for cell in range(BINS):
-                il, xl = cell // XL_DEV, cell % XL_DEV
-                if count == 8:
-                    out_ref[il, pl.ds(octet * 8 * XL_DEV + xl, 8, stride=XL_DEV), :] = value[cell]
-                else:
-                    row = octet * 8 * XL_DEV + xl
-                    out_ref[il, row:row + 1, :] = value[cell, :count, :]
+    split_store(bnewer, slice(0, BINS), jnp.concatenate(parts, axis=0))
+
+    eps = EPS * 81.0 * (radii_ref[jnp.clip(step - 2, 0, NBLK - 1)].astype(jnp.float32) + 1.0) ** 2
+
+    def smoothed(parts, band):
+        halves = jnp.concatenate([ref[half, rows, :] for ref, rows in parts for half in range(2)], axis=0)
+        whole = jnp.dot(halves, band, preferred_element_type=jnp.float32)
+        count = whole.shape[0] // (2 * len(parts))
+        return [
+            whole[2 * i * count:(2 * i + 1) * count] + whole[(2 * i + 1) * count:(2 * i + 2) * count]
+            for i in range(len(parts))
+        ]
+
+    def band_of(octet):
+        start = 40 - 8 * octet
+        return band_ref[0, (start // 8) % 2, start // 16 * 16:start // 16 * 16 + 2 * LANES, :]
+
+    bscale[...] = lax.rsqrt(smoothed([(bsmooth, slice(0, BINS))], band_of(3))[0] + eps)
+    for octet in range(OCT):
+        products(octet)
+        band = band_of(octet)
+        own_rows = slice(octet * 8 * BINS, (octet + 1) * 8 * BINS)
+        energy_rows = slice(OCT * 8 * BINS, (OCT + 1) * 8 * BINS)
+        cross, menergy = smoothed([(smooth, own_rows), (smooth, energy_rows)], band)
+        value = cross * lax.rsqrt(menergy + eps)
+        value = value.reshape(BINS, 8, LANES) * bscale[...].reshape(BINS, 1, LANES)
+        count = min(8, NLAG - 8 * octet)
+        for cell in range(BINS):
+            il, xl = cell // XL_DEV, cell % XL_DEV
+            if count == 8:
+                out_ref[il, pl.ds(octet * 8 * XL_DEV + xl, 8, stride=XL_DEV), :] = value[cell]
+            else:
+                row = octet * 8 * XL_DEV + xl
+                out_ref[il, row:row + 1, :] = value[cell, :count, :]
+    products(OCT)
+    for ref, fresh in ((smooth, newer), (bsmooth, bnewer)):
+        ref[:, :, :LANES] = ref[:, :, LANES:]
+        ref[:, :, LANES:] = fresh[...]
 
 
 def similarity(bm, bands, radii):
     out = pl.pallas_call(
         similarity_kernel,
-        grid=(NBLK + 1,),
+        grid=(NBLK + 2,),
         out_shape=jax.ShapeDtypeStruct((IL_DEV, NLAG * XL_DEV, NT), jnp.float32),
         in_specs=[
             pl.BlockSpec(memory_space=pltpu.SMEM),
             pl.BlockSpec((2, BINS_H, WIDE), lambda j: (0, 0, 0)),
-            pl.BlockSpec((1, 2, BAND, TBLK), lambda j: (jnp.maximum(j - 1, 0), 0, 0, 0)),
+            pl.BlockSpec((1, 2, BAND, TBLK), lambda j: (jnp.clip(j - 2, 0, NBLK - 1), 0, 0, 0)),
         ],
-        out_specs=pl.BlockSpec((IL_DEV, NLAG * XL_DEV, TBLK), lambda j: (0, 0, jnp.maximum(j - 1, 0))),
+        out_specs=pl.BlockSpec((IL_DEV, NLAG * XL_DEV, TBLK), lambda j: (0, 0, jnp.clip(j - 2, 0, NBLK - 1))),
         scratch_shapes=[
             pltpu.VMEM((OCT, BINS_H, LANES), jnp.float32),
             pltpu.VMEM((BINS_H, 8, LANES), jnp.float32),
             pltpu.VMEM((BINS_H, 8, LANES), jnp.float32),
             pltpu.VMEM((2, (OCT + 1) * 8 * BINS, 2 * LANES), jnp.bfloat16),
             pltpu.VMEM((2, BINS, 2 * LANES), jnp.bfloat16),
+            pltpu.VMEM((2, (OCT + 1) * 8 * BINS, LANES), jnp.bfloat16),
+            pltpu.VMEM((2, BINS, LANES), jnp.bfloat16),
             pltpu.VMEM((IL_DEV, 16, LANES), jnp.float32),
             pltpu.VMEM((BINS, LANES), jnp.float32),
         ],

time: 90.1 us -> 89.6 us (level)
  no operation moved by 1% of the time
where the time goes in v5:
time: 89.6 us; the launch traced here: 89.5 us
  Pallas kernels  83.8 us (94%)
  local copies, waits for them, and re-layouts  3.79 us (4%)
  other arithmetic  1.79 us (2%)
    pallas_call x1, Pallas kernels, haloed_stacks(): pl.pallas_call(functools.partial(stack_kernel, (chunks, nx, nz, ny)), out...  68.7 us
    pallas_call x1, Pallas kernels, similarity(): pl.pallas_call(similarity_kernel, grid=(NBLK + 2,), out_shape=jax.ShapeDt...  15.1 us
    unnamed x5, local copies, waits for them, and re-layouts  3.79 us

profile of v5, /device:TPU:1, one launch (start us, length us, event | category | flops | bytes accessed | tf_op | source)
XLA Modules:
  0.0 89.5 jit_solution(7234605590537113805)
XLA Ops:
  0.0 0.0 copy-start
  0.0 3.8 %copy.6 = bf16[1024,2,1536]{2,0,1:T(8,128)(2,1)S(1)} copy(bf16[1024,2,1536]{2,1,0:T(2,128)(2,1)} %param.3) | data formatting | bytes 12582912 | tf_op args[0]
  3.8 0.0 copy-done
  3.8 0.0 copy-start.1
  3.8 68.7 %stack.1.bm_ref = f32[2,72,1920]{2,1,0:T(8,128)S(1)} custom-call(s32[1,1024]{1,0:T(1,128)S(1)} %bitcast.8, bf16[2,1024,1536]{2,1,0:T(8,128)(2,1)S(1)} %bitcast.7), custom_call_target="tpu_custom_call" | custom-call | tf_op jit(solution)/shard_map/stack/pallas_call | solution.py:447
  72.5 0.1 add_add_fusion
  72.6 0.1 subtract_abs_fusion
  72.8 0.0 copy-done.1
  72.8 0.1 compare_and_fusion
  72.9 1.5 %select_convert_fusion.band_ref = bf16[12,2,288,128]{3,2,1,0:T(8,128)(2,1)S(1)} fusion(s32[2,288,128]{2,1,0:T(8,128)S(1)} %subtract_abs_fusion, s32[12]{0:T(128)S(1)} %broadcast_add_fusion, pred[12,2,288]{2,1,0:T(4,128)(4,1)S(1)} %compare_and_fusion), kind=kLoop, calls=%fused_computation.1 | loop fusion | flops 3538944 | bytes 2071344 | tf_op jit(solution)/shard_map/convert_element_type | solution.py:38
  74.4 15.1 %similarity.1 = f32[2,328,1536]{2,1,0:T(8,128)} custom-call(s32[12]{0:T(128)S(1)} %copy-done.1, f32[2,72,1920]{2,1,0:T(8,128)S(1)} %stack.1.bm_ref, bf16[12,2,288,128]{3,2,1,0:T(8,128)(2,1)S(1)} %select_convert_fusion.band_ref), custom_call_target="tpu_custom_call" | custom-call | tf_op jit(solution)/shard_map/similarity/pallas_call | solution.py:153
  (3 shorter events, 0.0 us)
Async XLA Ops:
  0.0 3.8 %copy-start = (s32[1024,1]{0,1:T(1,128)S(1)}, s32[1024,1]{0,1:T(1,128)}, u32[]{:S(2)}) copy-start(s32[1024,1]{0,1:T(1,128)} %param.4) | copy-start | bytes 12292
  3.8 69.0 %copy-start.1 = (s32[12]{0:T(128)S(1)}, s32[12]{0:T(128)}, u32[]{:S(2)}) copy-start(s32[12]{0:T(128)} %radii_ref.1) | copy-start | bytes 148
